TPU v7x, 256 devices: a whole 4x4x8 slice. The times are simulated.
256 devices in a mesh: depth: 8 (over x, core), tile: 32 (over z, y).
Axes of the slice: x: 4, y: 4, z: 8, core: 2. Of those that a mesh axis runs over, the one named last changes fastest.
Arguments:
- volume: bfloat16 [4096, 64, 64, 64], P(('depth', 'tile')), may hold values from 0.0099487305 to 0.5
- resampler: bfloat16 [2, 64, 128], replicated, may hold values from 0 to 1.4, as said below
- ramp_slope: float32 [3], replicated, may hold values from -12 to 12
- ramp_pivot: float32 [3], replicated, may hold values from 0.03 to 0.3
- tile_owner: int32 [4096, 2], P(('depth', 'tile')), may hold values from 0 to 31, all different within a row; in each aligned block of 16 rows (0 to 15, 16 to 31, ...) at most 2 rows name the same one
- tile_cell: int32 [4096, 2], P(('depth', 'tile')), may hold values from 0 to 7
- depth_order: int32 [2, 4096], P(None, ('depth', 'tile')), may hold values from 0 to 4095, each once within a row
- slab_rank: int32 [2, 8], replicated, may hold values from 0 to 7, each once within a row
Outputs:
- colour: float32 [2, 3, 32, 512, 128], P(None, None, 'tile', 'depth')
- transmittance: float32 [2, 32, 512, 128], P(None, 'tile', 'depth')
Inputs may be any that keep to these rules, and one draw needn't show every extreme that they name: `tile_owner`: each row names 2 different tile owners. Among the 16 rows of one device no owner is named by more than 2 rows, a bound that some block reaches. `depth_order`: each row is a permutation. `slab_rank`: each row is a permutation. `resampler`: nonnegative interpolation weights.
All inputs are finite; a program needn't handle non-finite values.
Results may differ from a plain program's by a relative error of at most 0.0025.
Values may be sent and summed in bfloat16 or wider, within the bound.
A program may use at most 128 MiB of HBM per device.

v0:
```python
import jax
import jax.numpy as jnp
from jax import lax
from jax.sharding import PartitionSpec as P

CELLS = 8


EXTINCTION = 1.0
TOP_PRECISION = lax.Precision.HIGHEST


def render_brick(brick, resampler, strict_lower, ramp_slope, ramp_pivot):
    rowwise_axis = jnp.einsum(
        "kri,is->krs", brick, resampler[0], preferred_element_type=jnp.float32
    )
    along_depth = jnp.einsum("rik,is->krs", brick, resampler[1], preferred_element_type=jnp.float32)
    samples = jnp.stack([rowwise_axis, along_depth])
    optical = samples * (EXTINCTION / samples.shape[1])
    nearest_depth = jnp.einsum("kj,vjrs->vkrs", strict_lower, optical, precision=TOP_PRECISION)
    weight = jnp.exp(-nearest_depth) * (1.0 - jnp.exp(-optical))
    layers = []
    for channel in range(3):
        tinted = jax.nn.sigmoid(ramp_slope[channel] * (samples - ramp_pivot[channel]))
        layers.append(jnp.sum(weight * tinted, axis=1))
    layers.append(jnp.sum(optical, axis=1))
    return jnp.stack(layers, axis=1)


def bucket_slots(targets):
    positions = jnp.arange(targets.shape[0])
    earlier = (targets[None, :] == targets[:, None]) & (positions[None, :] < positions[:, None])
    return jnp.sum(earlier.astype(jnp.int32), axis=1)


def compose(received, filled, view_tag, cell_tag, rank_tag, view_count):
    slot_count, _, brick_rows, sample_cols = received.shape
    before = filled[None, :] & (view_tag[None, :] == view_tag[:, None])
    before = (
        before & (cell_tag[None, :] == cell_tag[:, None]) & (rank_tag[None, :] < rank_tag[:, None])
    )
    depth_values = received[:, 3].reshape(slot_count, brick_rows * sample_cols)
    nearest_depth = jnp.dot(before.astype(jnp.float32), depth_values, precision=TOP_PRECISION)
    nearest_depth = nearest_depth.reshape(slot_count, brick_rows, sample_cols)
    lit_colour = received[:, :3] * jnp.exp(-nearest_depth)[:, None]
    view_ids = jnp.arange(view_count, dtype=jnp.int32)
    cell_ids = jnp.arange(CELLS, dtype=jnp.int32)
    selector = filled[None, None, :] & (view_tag[None, None, :] == view_ids[:, None, None])
    selector = (selector & (cell_tag[None, None, :] == cell_ids[None, :, None])).astype(jnp.float32)
    colour = jnp.einsum("vcq,qxrw->vxcrw", selector, lit_colour, precision=TOP_PRECISION)
    optical_total = jnp.einsum("vcq,qrw->vcrw", selector, received[:, 3], precision=TOP_PRECISION)
    tile_rows = CELLS * brick_rows
    colour = colour.reshape(view_count, 3, tile_rows, sample_cols)
    optical_total = optical_total.reshape(view_count, 1, tile_rows, sample_cols)
    return jnp.concatenate([colour, optical_total], axis=1).astype(jnp.bfloat16)


def blend_slabs(stacked, slab_rank):
    is_nearer = (slab_rank[:, None, :] < slab_rank[:, :, None]).astype(jnp.float32)
    depth_values = stacked[:, :, 3]
    nearest_depth = jnp.einsum("ksz,zkoh->skoh", is_nearer, depth_values, precision=TOP_PRECISION)
    colour = jnp.sum(jnp.exp(-nearest_depth)[:, :, None] * stacked[:, :, :3], axis=0)
    transmit = jnp.exp(-jnp.sum(depth_values, axis=0))
    return (colour, transmit)


def body(volume, resampler, ramp_slope, ramp_pivot, tile_owner, tile_cell, depth_order, slab_rank):
    brick_count = volume.shape[0]
    brick_edge = volume.shape[1]
    sample_cols = resampler.shape[2]
    view_count = resampler.shape[0]
    tile_count = lax.axis_size("tile")
    capacity = max(2, 2 * view_count * brick_count // tile_count)
    edge_ids = jnp.arange(brick_edge)
    strict_lower = (edge_ids[None, :] < edge_ids[:, None]).astype(jnp.float32)
    prints = lax.map(
        lambda brick: render_brick(brick, resampler, strict_lower, ramp_slope, ramp_pivot), volume
    )
    slot_total = tile_count * capacity
    targets = tile_owner.reshape(-1)
    slot_index = bucket_slots(targets)
    flat_prints = prints.reshape(brick_count * view_count, 4, brick_edge, sample_cols)
    view_tags = jnp.tile(jnp.arange(view_count, dtype=jnp.int32), brick_count)
    label_values = jnp.stack(
        [jnp.ones_like(targets), view_tags, tile_cell.reshape(-1), depth_order.T.reshape(-1)],
        axis=1,
    )
    buffer = jnp.zeros((tile_count, capacity, 4, brick_edge, sample_cols), jnp.float32)
    buffer = buffer.at[targets, slot_index].set(flat_prints)
    slot_tags = (
        jnp.zeros((tile_count, capacity, 4), jnp.int32).at[targets, slot_index].set(label_values)
    )
    received, got_tags = (
        lax.all_to_all(buffer, "tile", split_axis=0, concat_axis=0, tiled=True),
        lax.all_to_all(slot_tags, "tile", split_axis=0, concat_axis=0, tiled=True),
    )
    received = received.reshape(slot_total, 4, brick_edge, sample_cols)
    got_tags = got_tags.reshape(slot_total, 4)
    slab_tile_piece = compose(
        received, got_tags[:, 0] == 1, got_tags[:, 1], got_tags[:, 2], got_tags[:, 3], view_count
    )
    row_bands = lax.all_to_all(
        slab_tile_piece[None], "depth", split_axis=3, concat_axis=0, tiled=True
    ).astype(jnp.float32)
    colour, transmit = blend_slabs(row_bands, slab_rank)
    return (colour[:, :, None], transmit[:, None])


def solution(mesh):
    in_specs = (
        P(("depth", "tile"), None, None, None),
        P(),
        P(),
        P(),
        P(("depth", "tile"), None),
        P(("depth", "tile"), None),
        P(None, ("depth", "tile")),
        P(),
    )
    out_specs = (P(None, None, "tile", "depth", None), P(None, "tile", "depth", None))
    return jax.shard_map(body, mesh=mesh, in_specs=in_specs, out_specs=out_specs, check_vma=False)
```

profile of v0, /device:TPU:33, one launch (start us, length us, event | category | flops | bytes accessed | tf_op | source)
XLA Modules:
  0.0 634.6 jit_solution(16208095654835917297)
XLA Ops:
  4.3 3.9 scatter_fusion.1
  8.2 10.8 %all-to-all-start.1 = ((s32[32,2,4]{2,1,0:T(2,128)}), s32[32,2,4]{2,1,0:T(2,128)S(1)}, u32[]{:S(2)}, u32[]{:S(2)}) async-start(s32[32,2,4]{2,1,0:T(2,128)} %scatter_fusion.1), calls=%async_computation.1 | async-start | bytes 65536 | tf_op jit(solution)/shard_map/all_to_all | solution.py:95
  19.0 362.4 %while.11 = (s32[]{:T(128)}, f32[16,2,4,64,128]{4,3,2,1,0:T(8,128)}, bf16[16,64,64,64]{3,2,1,0:T(8,128)(2,1)}, bf16[2,64,128]{2,1,0:T(8,128)(2,1)}, f32[3]{0:T(128)}, /*index=5*/f32[3]{0:T(128)}, s32[]{:T(128)}) while((s32[]{:T(128)}, f32[16,2,4,64,128]{4,3,2,1,0:T(8,128)}, bf16[16,64,64,64]{3,2,1,0:T(8,128)(2,1)}, ...), condition=%wide.region_6.7_spmd.clone, body=%wide.region_1.6_spmd.clone.sunk | while | flops 971120640 | bytes 34504896 | solution.py:76
  21.8 1.6 copy.138
  25.1 6.6 %fusion.82 = f32[2,64,128,64]{2,3,1,0:T(8,128)S(1)} fusion(f32[2,64,64,128]{3,2,1,0:T(8,128)S(1)} %broadcast_multiply_fusion.2), kind=kOutput, calls=%fused_computation.7.clone.1 | convolution fusion | flops 805314560 | bytes 8388608 | tf_op jit(solution)/shard_map/while/body/eval_jaxpr/kj,vjrs->vkrs/dot_general | solution.py:20
  31.7 9.3 %multiply_reduce_fusion.5 = (f32[2,64,128]{2,1,0:T(8,128)S(1)}, f32[2,64,128]{2,1,0:T(8,128)S(1)}, f32[2,64,128]{2,1,0:T(8,128)S(1)}, f32[2,64,128]{2,1,0:T(8,128)S(1)}) fusion(f32[2,64,128,64]{2,3,1,0:T(8,128)S(1)} %fusion.82, f32[]{:T(128)} %bitcast.156, f32[]{:T(128)} %bitcast.157, f32[1,64,64,128]{3,2,1,0:T(8,128)S(1)} %convolution_bitcast_fusion.4, ...), kind=kLoop, calls=%fused_computation.11.clone.1 | loop fusion | flops 29294592 | bytes 8650776 | tf_op jit(solution)/shard_map/while/body/eval_jaxpr/reduce_sum | solution.py:25
  47.7 6.6 %fusion.82 = f32[2,64,128,64]{2,3,1,0:T(8,128)S(1)} fusion(f32[2,64,64,128]{3,2,1,0:T(8,128)S(1)} %broadcast_multiply_fusion.2), kind=kOutput, calls=%fused_computation.7.clone.1 | convolution fusion | flops 805314560 | bytes 8388608 | tf_op jit(solution)/shard_map/while/body/eval_jaxpr/kj,vjrs->vkrs/dot_general | solution.py:20
  54.3 9.3 %multiply_reduce_fusion.5 = (f32[2,64,128]{2,1,0:T(8,128)S(1)}, f32[2,64,128]{2,1,0:T(8,128)S(1)}, f32[2,64,128]{2,1,0:T(8,128)S(1)}, f32[2,64,128]{2,1,0:T(8,128)S(1)}) fusion(f32[2,64,128,64]{2,3,1,0:T(8,128)S(1)} %fusion.82, f32[]{:T(128)} %bitcast.156, f32[]{:T(128)} %bitcast.157, f32[1,64,64,128]{3,2,1,0:T(8,128)S(1)} %convolution_bitcast_fusion.4, ...), kind=kLoop, calls=%fused_computation.11.clone.1 | loop fusion | flops 29294592 | bytes 8650776 | tf_op jit(solution)/shard_map/while/body/eval_jaxpr/reduce_sum | solution.py:25
  67.0 1.6 copy.138
  70.3 6.6 %fusion.82 = f32[2,64,128,64]{2,3,1,0:T(8,128)S(1)} fusion(f32[2,64,64,128]{3,2,1,0:T(8,128)S(1)} %broadcast_multiply_fusion.2), kind=kOutput, calls=%fused_computation.7.clone.1 | convolution fusion | flops 805314560 | bytes 8388608 | tf_op jit(solution)/shard_map/while/body/eval_jaxpr/kj,vjrs->vkrs/dot_general | solution.py:20
  76.9 9.3 %multiply_reduce_fusion.5 = (f32[2,64,128]{2,1,0:T(8,128)S(1)}, f32[2,64,128]{2,1,0:T(8,128)S(1)}, f32[2,64,128]{2,1,0:T(8,128)S(1)}, f32[2,64,128]{2,1,0:T(8,128)S(1)}) fusion(f32[2,64,128,64]{2,3,1,0:T(8,128)S(1)} %fusion.82, f32[]{:T(128)} %bitcast.156, f32[]{:T(128)} %bitcast.157, f32[1,64,64,128]{3,2,1,0:T(8,128)S(1)} %convolution_bitcast_fusion.4, ...), kind=kLoop, calls=%fused_computation.11.clone.1 | loop fusion | flops 29294592 | bytes 8650776 | tf_op jit(solution)/shard_map/while/body/eval_jaxpr/reduce_sum | solution.py:25
  93.0 6.6 %fusion.82 = f32[2,64,128,64]{2,3,1,0:T(8,128)S(1)} fusion(f32[2,64,64,128]{3,2,1,0:T(8,128)S(1)} %broadcast_multiply_fusion.2), kind=kOutput, calls=%fused_computation.7.clone.1 | convolution fusion | flops 805314560 | bytes 8388608 | tf_op jit(solution)/shard_map/while/body/eval_jaxpr/kj,vjrs->vkrs/dot_general | solution.py:20
  99.6 9.3 %multiply_reduce_fusion.5 = (f32[2,64,128]{2,1,0:T(8,128)S(1)}, f32[2,64,128]{2,1,0:T(8,128)S(1)}, f32[2,64,128]{2,1,0:T(8,128)S(1)}, f32[2,64,128]{2,1,0:T(8,128)S(1)}) fusion(f32[2,64,128,64]{2,3,1,0:T(8,128)S(1)} %fusion.82, f32[]{:T(128)} %bitcast.156, f32[]{:T(128)} %bitcast.157, f32[1,64,64,128]{3,2,1,0:T(8,128)S(1)} %convolution_bitcast_fusion.4, ...), kind=kLoop, calls=%fused_computation.11.clone.1 | loop fusion | flops 29294592 | bytes 8650776 | tf_op jit(solution)/shard_map/while/body/eval_jaxpr/reduce_sum | solution.py:25
  115.7 6.6 %fusion.82 = f32[2,64,128,64]{2,3,1,0:T(8,128)S(1)} fusion(f32[2,64,64,128]{3,2,1,0:T(8,128)S(1)} %broadcast_multiply_fusion.2), kind=kOutput, calls=%fused_computation.7.clone.1 | convolution fusion | flops 805314560 | bytes 8388608 | tf_op jit(solution)/shard_map/while/body/eval_jaxpr/kj,vjrs->vkrs/dot_general | solution.py:20
  122.3 9.3 %multiply_reduce_fusion.5 = (f32[2,64,128]{2,1,0:T(8,128)S(1)}, f32[2,64,128]{2,1,0:T(8,128)S(1)}, f32[2,64,128]{2,1,0:T(8,128)S(1)}, f32[2,64,128]{2,1,0:T(8,128)S(1)}) fusion(f32[2,64,128,64]{2,3,1,0:T(8,128)S(1)} %fusion.82, f32[]{:T(128)} %bitcast.156, f32[]{:T(128)} %bitcast.157, f32[1,64,64,128]{3,2,1,0:T(8,128)S(1)} %convolution_bitcast_fusion.4, ...), kind=kLoop, calls=%fused_computation.11.clone.1 | loop fusion | flops 29294592 | bytes 8650776 | tf_op jit(solution)/shard_map/while/body/eval_jaxpr/reduce_sum | solution.py:25
  138.3 6.6 %fusion.82 = f32[2,64,128,64]{2,3,1,0:T(8,128)S(1)} fusion(f32[2,64,64,128]{3,2,1,0:T(8,128)S(1)} %broadcast_multiply_fusion.2), kind=kOutput, calls=%fused_computation.7.clone.1 | convolution fusion | flops 805314560 | bytes 8388608 | tf_op jit(solution)/shard_map/while/body/eval_jaxpr/kj,vjrs->vkrs/dot_general | solution.py:20
  144.9 9.3 %multiply_reduce_fusion.5 = (f32[2,64,128]{2,1,0:T(8,128)S(1)}, f32[2,64,128]{2,1,0:T(8,128)S(1)}, f32[2,64,128]{2,1,0:T(8,128)S(1)}, f32[2,64,128]{2,1,0:T(8,128)S(1)}) fusion(f32[2,64,128,64]{2,3,1,0:T(8,128)S(1)} %fusion.82, f32[]{:T(128)} %bitcast.156, f32[]{:T(128)} %bitcast.157, f32[1,64,64,128]{3,2,1,0:T(8,128)S(1)} %convolution_bitcast_fusion.4, ...), kind=kLoop, calls=%fused_computation.11.clone.1 | loop fusion | flops 29294592 | bytes 8650776 | tf_op jit(solution)/shard_map/while/body/eval_jaxpr/reduce_sum | solution.py:25
  161.0 6.6 %fusion.82 = f32[2,64,128,64]{2,3,1,0:T(8,128)S(1)} fusion(f32[2,64,64,128]{3,2,1,0:T(8,128)S(1)} %broadcast_multiply_fusion.2), kind=kOutput, calls=%fused_computation.7.clone.1 | convolution fusion | flops 805314560 | bytes 8388608 | tf_op jit(solution)/shard_map/while/body/eval_jaxpr/kj,vjrs->vkrs/dot_general | solution.py:20
  167.6 9.3 %multiply_reduce_fusion.5 = (f32[2,64,128]{2,1,0:T(8,128)S(1)}, f32[2,64,128]{2,1,0:T(8,128)S(1)}, f32[2,64,128]{2,1,0:T(8,128)S(1)}, f32[2,64,128]{2,1,0:T(8,128)S(1)}) fusion(f32[2,64,128,64]{2,3,1,0:T(8,128)S(1)} %fusion.82, f32[]{:T(128)} %bitcast.156, f32[]{:T(128)} %bitcast.157, f32[1,64,64,128]{3,2,1,0:T(8,128)S(1)} %convolution_bitcast_fusion.4, ...), kind=kLoop, calls=%fused_computation.11.clone.1 | loop fusion | flops 29294592 | bytes 8650776 | tf_op jit(solution)/shard_map/while/body/eval_jaxpr/reduce_sum | solution.py:25
  183.6 6.6 %fusion.82 = f32[2,64,128,64]{2,3,1,0:T(8,128)S(1)} fusion(f32[2,64,64,128]{3,2,1,0:T(8,128)S(1)} %broadcast_multiply_fusion.2), kind=kOutput, calls=%fused_computation.7.clone.1 | convolution fusion | flops 805314560 | bytes 8388608 | tf_op jit(solution)/shard_map/while/body/eval_jaxpr/kj,vjrs->vkrs/dot_general | solution.py:20
  190.2 9.3 %multiply_reduce_fusion.5 = (f32[2,64,128]{2,1,0:T(8,128)S(1)}, f32[2,64,128]{2,1,0:T(8,128)S(1)}, f32[2,64,128]{2,1,0:T(8,128)S(1)}, f32[2,64,128]{2,1,0:T(8,128)S(1)}) fusion(f32[2,64,128,64]{2,3,1,0:T(8,128)S(1)} %fusion.82, f32[]{:T(128)} %bitcast.156, f32[]{:T(128)} %bitcast.157, f32[1,64,64,128]{3,2,1,0:T(8,128)S(1)} %convolution_bitcast_fusion.4, ...), kind=kLoop, calls=%fused_computation.11.clone.1 | loop fusion | flops 29294592 | bytes 8650776 | tf_op jit(solution)/shard_map/while/body/eval_jaxpr/reduce_sum | solution.py:25
  206.2 6.6 %fusion.82 = f32[2,64,128,64]{2,3,1,0:T(8,128)S(1)} fusion(f32[2,64,64,128]{3,2,1,0:T(8,128)S(1)} %broadcast_multiply_fusion.2), kind=kOutput, calls=%fused_computation.7.clone.1 | convolution fusion | flops 805314560 | bytes 8388608 | tf_op jit(solution)/shard_map/while/body/eval_jaxpr/kj,vjrs->vkrs/dot_general | solution.py:20
  212.9 9.3 %multiply_reduce_fusion.5 = (f32[2,64,128]{2,1,0:T(8,128)S(1)}, f32[2,64,128]{2,1,0:T(8,128)S(1)}, f32[2,64,128]{2,1,0:T(8,128)S(1)}, f32[2,64,128]{2,1,0:T(8,128)S(1)}) fusion(f32[2,64,128,64]{2,3,1,0:T(8,128)S(1)} %fusion.82, f32[]{:T(128)} %bitcast.156, f32[]{:T(128)} %bitcast.157, f32[1,64,64,128]{3,2,1,0:T(8,128)S(1)} %convolution_bitcast_fusion.4, ...), kind=kLoop, calls=%fused_computation.11.clone.1 | loop fusion | flops 29294592 | bytes 8650776 | tf_op jit(solution)/shard_map/while/body/eval_jaxpr/reduce_sum | solution.py:25
  225.6 1.6 copy.138
  228.9 6.6 %fusion.82 = f32[2,64,128,64]{2,3,1,0:T(8,128)S(1)} fusion(f32[2,64,64,128]{3,2,1,0:T(8,128)S(1)} %broadcast_multiply_fusion.2), kind=kOutput, calls=%fused_computation.7.clone.1 | convolution fusion | flops 805314560 | bytes 8388608 | tf_op jit(solution)/shard_map/while/body/eval_jaxpr/kj,vjrs->vkrs/dot_general | solution.py:20
  235.5 9.3 %multiply_reduce_fusion.5 = (f32[2,64,128]{2,1,0:T(8,128)S(1)}, f32[2,64,128]{2,1,0:T(8,128)S(1)}, f32[2,64,128]{2,1,0:T(8,128)S(1)}, f32[2,64,128]{2,1,0:T(8,128)S(1)}) fusion(f32[2,64,128,64]{2,3,1,0:T(8,128)S(1)} %fusion.82, f32[]{:T(128)} %bitcast.156, f32[]{:T(128)} %bitcast.157, f32[1,64,64,128]{3,2,1,0:T(8,128)S(1)} %convolution_bitcast_fusion.4, ...), kind=kLoop, calls=%fused_computation.11.clone.1 | loop fusion | flops 29294592 | bytes 8650776 | tf_op jit(solution)/shard_map/while/body/eval_jaxpr/reduce_sum | solution.py:25
  251.6 6.6 %fusion.82 = f32[2,64,128,64]{2,3,1,0:T(8,128)S(1)} fusion(f32[2,64,64,128]{3,2,1,0:T(8,128)S(1)} %broadcast_multiply_fusion.2), kind=kOutput, calls=%fused_computation.7.clone.1 | convolution fusion | flops 805314560 | bytes 8388608 | tf_op jit(solution)/shard_map/while/body/eval_jaxpr/kj,vjrs->vkrs/dot_general | solution.py:20
  258.2 9.3 %multiply_reduce_fusion.5 = (f32[2,64,128]{2,1,0:T(8,128)S(1)}, f32[2,64,128]{2,1,0:T(8,128)S(1)}, f32[2,64,128]{2,1,0:T(8,128)S(1)}, f32[2,64,128]{2,1,0:T(8,128)S(1)}) fusion(f32[2,64,128,64]{2,3,1,0:T(8,128)S(1)} %fusion.82, f32[]{:T(128)} %bitcast.156, f32[]{:T(128)} %bitcast.157, f32[1,64,64,128]{3,2,1,0:T(8,128)S(1)} %convolution_bitcast_fusion.4, ...), kind=kLoop, calls=%fused_computation.11.clone.1 | loop fusion | flops 29294592 | bytes 8650776 | tf_op jit(solution)/shard_map/while/body/eval_jaxpr/reduce_sum | solution.py:25
  274.2 6.6 %fusion.82 = f32[2,64,128,64]{2,3,1,0:T(8,128)S(1)} fusion(f32[2,64,64,128]{3,2,1,0:T(8,128)S(1)} %broadcast_multiply_fusion.2), kind=kOutput, calls=%fused_computation.7.clone.1 | convolution fusion | flops 805314560 | bytes 8388608 | tf_op jit(solution)/shard_map/while/body/eval_jaxpr/kj,vjrs->vkrs/dot_general | solution.py:20
  280.8 9.3 %multiply_reduce_fusion.5 = (f32[2,64,128]{2,1,0:T(8,128)S(1)}, f32[2,64,128]{2,1,0:T(8,128)S(1)}, f32[2,64,128]{2,1,0:T(8,128)S(1)}, f32[2,64,128]{2,1,0:T(8,128)S(1)}) fusion(f32[2,64,128,64]{2,3,1,0:T(8,128)S(1)} %fusion.82, f32[]{:T(128)} %bitcast.156, f32[]{:T(128)} %bitcast.157, f32[1,64,64,128]{3,2,1,0:T(8,128)S(1)} %convolution_bitcast_fusion.4, ...), kind=kLoop, calls=%fused_computation.11.clone.1 | loop fusion | flops 29294592 | bytes 8650776 | tf_op jit(solution)/shard_map/while/body/eval_jaxpr/reduce_sum | solution.py:25
  296.8 6.6 %fusion.82 = f32[2,64,128,64]{2,3,1,0:T(8,128)S(1)} fusion(f32[2,64,64,128]{3,2,1,0:T(8,128)S(1)} %broadcast_multiply_fusion.2), kind=kOutput, calls=%fused_computation.7.clone.1 | convolution fusion | flops 805314560 | bytes 8388608 | tf_op jit(solution)/shard_map/while/body/eval_jaxpr/kj,vjrs->vkrs/dot_general | solution.py:20
  303.4 9.3 %multiply_reduce_fusion.5 = (f32[2,64,128]{2,1,0:T(8,128)S(1)}, f32[2,64,128]{2,1,0:T(8,128)S(1)}, f32[2,64,128]{2,1,0:T(8,128)S(1)}, f32[2,64,128]{2,1,0:T(8,128)S(1)}) fusion(f32[2,64,128,64]{2,3,1,0:T(8,128)S(1)} %fusion.82, f32[]{:T(128)} %bitcast.156, f32[]{:T(128)} %bitcast.157, f32[1,64,64,128]{3,2,1,0:T(8,128)S(1)} %convolution_bitcast_fusion.4, ...), kind=kLoop, calls=%fused_computation.11.clone.1 | loop fusion | flops 29294592 | bytes 8650776 | tf_op jit(solution)/shard_map/while/body/eval_jaxpr/reduce_sum | solution.py:25
  319.5 6.6 %fusion.82 = f32[2,64,128,64]{2,3,1,0:T(8,128)S(1)} fusion(f32[2,64,64,128]{3,2,1,0:T(8,128)S(1)} %broadcast_multiply_fusion.2), kind=kOutput, calls=%fused_computation.7.clone.1 | convolution fusion | flops 805314560 | bytes 8388608 | tf_op jit(solution)/shard_map/while/body/eval_jaxpr/kj,vjrs->vkrs/dot_general | solution.py:20
  326.1 9.3 %multiply_reduce_fusion.5 = (f32[2,64,128]{2,1,0:T(8,128)S(1)}, f32[2,64,128]{2,1,0:T(8,128)S(1)}, f32[2,64,128]{2,1,0:T(8,128)S(1)}, f32[2,64,128]{2,1,0:T(8,128)S(1)}) fusion(f32[2,64,128,64]{2,3,1,0:T(8,128)S(1)} %fusion.82, f32[]{:T(128)} %bitcast.156, f32[]{:T(128)} %bitcast.157, f32[1,64,64,128]{3,2,1,0:T(8,128)S(1)} %convolution_bitcast_fusion.4, ...), kind=kLoop, calls=%fused_computation.11.clone.1 | loop fusion | flops 29294592 | bytes 8650776 | tf_op jit(solution)/shard_map/while/body/eval_jaxpr/reduce_sum | solution.py:25
  338.8 1.6 copy.138
  342.1 6.6 %fusion.82 = f32[2,64,128,64]{2,3,1,0:T(8,128)S(1)} fusion(f32[2,64,64,128]{3,2,1,0:T(8,128)S(1)} %broadcast_multiply_fusion.2), kind=kOutput, calls=%fused_computation.7.clone.1 | convolution fusion | flops 805314560 | bytes 8388608 | tf_op jit(solution)/shard_map/while/body/eval_jaxpr/kj,vjrs->vkrs/dot_general | solution.py:20
  348.7 9.3 %multiply_reduce_fusion.5 = (f32[2,64,128]{2,1,0:T(8,128)S(1)}, f32[2,64,128]{2,1,0:T(8,128)S(1)}, f32[2,64,128]{2,1,0:T(8,128)S(1)}, f32[2,64,128]{2,1,0:T(8,128)S(1)}) fusion(f32[2,64,128,64]{2,3,1,0:T(8,128)S(1)} %fusion.82, f32[]{:T(128)} %bitcast.156, f32[]{:T(128)} %bitcast.157, f32[1,64,64,128]{3,2,1,0:T(8,128)S(1)} %convolution_bitcast_fusion.4, ...), kind=kLoop, calls=%fused_computation.11.clone.1 | loop fusion | flops 29294592 | bytes 8650776 | tf_op jit(solution)/shard_map/while/body/eval_jaxpr/reduce_sum | solution.py:25
  361.5 1.6 copy.138
  364.8 6.6 %fusion.82 = f32[2,64,128,64]{2,3,1,0:T(8,128)S(1)} fusion(f32[2,64,64,128]{3,2,1,0:T(8,128)S(1)} %broadcast_multiply_fusion.2), kind=kOutput, calls=%fused_computation.7.clone.1 | convolution fusion | flops 805314560 | bytes 8388608 | tf_op jit(solution)/shard_map/while/body/eval_jaxpr/kj,vjrs->vkrs/dot_general | solution.py:20
  371.4 9.3 %multiply_reduce_fusion.5 = (f32[2,64,128]{2,1,0:T(8,128)S(1)}, f32[2,64,128]{2,1,0:T(8,128)S(1)}, f32[2,64,128]{2,1,0:T(8,128)S(1)}, f32[2,64,128]{2,1,0:T(8,128)S(1)}) fusion(f32[2,64,128,64]{2,3,1,0:T(8,128)S(1)} %fusion.82, f32[]{:T(128)} %bitcast.156, f32[]{:T(128)} %bitcast.157, f32[1,64,64,128]{3,2,1,0:T(8,128)S(1)} %convolution_bitcast_fusion.4, ...), kind=kLoop, calls=%fused_computation.11.clone.1 | loop fusion | flops 29294592 | bytes 8650776 | tf_op jit(solution)/shard_map/while/body/eval_jaxpr/reduce_sum | solution.py:25
  381.4 4.3 broadcast_in_dim.12
  385.7 8.6 %scatter_fusion = f32[32,2,4,64,128]{4,3,2,1,0:T(8,128)} fusion(f32[32,2,4,64,128]{4,3,2,1,0:T(8,128)} %broadcast_in_dim.12, s32[32]{0:T(128)S(1)} %fusion.60, f32[32,4,64,128]{3,2,1,0:T(8,128)} %bitcast.172), kind=kCustom, calls=%fused_computation | custom fusion | bytes 12583168 | tf_op jit(solution)/shard_map/scatter | solution.py:89
  394.3 9.4 %all-to-all-start = ((f32[32,2,4,64,128]{4,3,2,1,0:T(8,128)}), f32[32,2,4,64,128]{4,3,2,1,0:T(8,128)}, u32[]{:S(2)}, u32[]{:S(2)}) async-start(f32[32,2,4,64,128]{4,3,2,1,0:T(8,128)} %scatter_fusion), calls=%async_computation | async-start | bytes 16777216 | tf_op jit(solution)/shard_map/all_to_all | solution.py:94
  404.0 179.9 %all-to-all-done = f32[32,2,4,64,128]{4,3,2,1,0:T(8,128)} async-done(((f32[32,2,4,64,128]{4,3,2,1,0:T(8,128)}), f32[32,2,4,64,128]{4,3,2,1,0:T(8,128)}, u32[]{:S(2)}, u32[]{:S(2)}) %all-to-all-start) | async-done | bytes 8388640 | tf_op jit(solution)/shard_map/all_to_all | solution.py:94
  583.9 14.4 %copy.86 = f32[32,2,4,64,128]{4,1,0,3,2:T(2,128)S(1)} copy(f32[32,2,4,64,128]{4,3,2,1,0:T(8,128)} %all-to-all-done) | data formatting | bytes 16777216 | tf_op jit(solution)/shard_map/all_to_all | solution.py:94
  600.6 2.6 negate_exponential_fusion
  603.3 2.5 fusion.27
  606.9 24.7 %all_to_all.28 = bf16[1,2,4,512,128]{4,2,1,0,3:T(4,128)(2,1)S(1)} all-to-all(bf16[1,2,4,512,128]{4,2,1,0,3:T(4,128)(2,1)S(1)} %copy.95), channel_id=1, replica_groups=mesh['depth'=8,'tile'=32] {'depth'}, dimensions={3} | all-to-all | bytes 2097152 | tf_op jit(solution)/shard_map/all_to_all | solution.py:102
  (175 shorter events, 110.3 us)
Async XLA Ops:
  8.2 386.1 %all-to-all-start.1 = ((s32[32,2,4]{2,1,0:T(2,128)}), s32[32,2,4]{2,1,0:T(2,128)S(1)}, u32[]{:S(2)}, u32[]{:S(2)}) async-start(s32[32,2,4]{2,1,0:T(2,128)} %scatter_fusion.1), calls=%async_computation.1 | async-start | bytes 65536 | tf_op jit(solution)/shard_map/all_to_all | solution.py:95
  19.0 4.4 copy-start
  41.7 4.4 copy-start
  64.3 4.4 copy-start
  87.0 4.4 copy-start
  109.6 4.4 copy-start
  132.3 4.4 copy-start
  154.9 4.4 copy-start
  177.6 4.4 copy-start
  200.2 4.4 copy-start
  222.9 4.4 copy-start
  245.5 4.4 copy-start
  268.2 4.4 copy-start
  290.8 4.4 copy-start
  313.4 4.4 copy-start
  336.1 4.4 copy-start
  358.7 4.4 copy-start
  394.3 189.6 %all-to-all-start = ((f32[32,2,4,64,128]{4,3,2,1,0:T(8,128)}), f32[32,2,4,64,128]{4,3,2,1,0:T(8,128)}, u32[]{:S(2)}, u32[]{:S(2)}) async-start(f32[32,2,4,64,128]{4,3,2,1,0:T(8,128)} %scatter_fusion), calls=%async_computation | async-start | bytes 16777216 | tf_op jit(solution)/shard_map/all_to_all | solution.py:94
  606.0 26.3 %copy-start.1 = (s32[2,8]{1,0:T(2,128)S(1)}, s32[2,8]{1,0:T(2,128)}, u32[]{:S(2)}) copy-start(s32[2,8]{1,0:T(2,128)} %param.17) | copy-start | bytes 196
where the time goes:
time: 645 us; the launch traced here: 635 us
  waiting for transfers between devices  180 us (28%)
  other arithmetic  176 us (27%)
  matrix products  125 us (19%)
  local copies, waits for them, and re-layouts  108 us (17%)
  blocking collectives  24.7 us (4%)
  starting transfers between devices  20.2 us (3%)
    all_to_all x1, waiting for transfers between devices, body(): lax.all_to_all(buffer, 'tile', split_axis=0, concat_axis=0, tiled=True)  180 us
    reduce_sum x16, other arithmetic, render_brick(): layers.append(jnp.sum(weight * tinted, axis=1))  148 us
    dot_general x16, matrix products, render_brick(): jnp.einsum('kj,vjrs->vkrs', strict_lower, optical, precision=TOP_PRECISION)  106 us
    squeeze x32, local copies, waits for them, and re-layouts, body(): lax.map(lambda brick: render_brick(brick, resampler, strict_lower, ramp_s...  46.6 us
    all_to_all x1, blocking collectives, body(): lax.all_to_all(slab_tile_piece[None], 'depth', split_axis=3, concat_axis=...  24.7 us
    slice x16, local copies, waits for them, and re-layouts, render_brick(): ramp_slope[channel] * (samples - ramp_pivot[channel])  23.2 us
    all_to_all x1, local copies, waits for them, and re-layouts, body(): lax.all_to_all(buffer, 'tile', split_axis=0, concat_axis=0, tiled=True)  14.4 us
    mul x16, other arithmetic, render_brick(): optical = samples * (EXTINCTION / samples.shape[1])  13.3 us
  transfers between devices with their start and end apart: 2, of which 1 were waited for; matrix products, arithmetic and copies ran while one was open for 59% of the time, Pallas kernels for 0%

commit v1 on v0

v1 whole, which is shorter than its diff:
```python
import jax
import jax.numpy as jnp
from jax import lax
from jax.experimental import pallas as pl
from jax.experimental.pallas import tpu as pltpu
from jax.sharding import PartitionSpec as P

BF = jnp.bfloat16
F32 = jnp.float32
CELLS = 8
ROWS = 64
COLS = 128
BRICKS = 16
OWNERS = 32
SLOTS = 64
RC = 16
CHUNKS = ROWS // RC
EXP_SCALE = -1.4426950408889634 / 64.0


def march(samples_of, coef, write):
    zero = jnp.zeros((RC, COLS), F32)

    def step(block, carry):
        front, light, a0, a1, a2 = carry
        acc = [a0, a1, a2]
        rows = samples_of(block)
        for j in range(8):
            s = rows[j]
            front = front + s
            after = jnp.exp2(front * EXP_SCALE)
            weight = light - after
            light = after
            for c in range(3):
                acc[c] = acc[c] + weight * jnp.tanh(s * coef[c][0] + coef[c][1])
        return (front, light, *acc)

    front, light, a0, a1, a2 = lax.fori_loop(0, 8, step, (zero, zero + 1.0, zero, zero, zero), unroll=8)
    total = 1.0 - light
    for c, acc in enumerate((a0, a1, a2)):
        write(c, (0.5 * (total + acc)).astype(BF))
    write(3, (front * (1.0 / 64.0)).astype(BF))


def render_kernel(place, slope, pivot, res0, res1, vol0, vol1, out, samples):
    coef = []
    for c in range(3):
        half = slope[c] * 0.5
        coef.append((half, -half * pivot[c]))
    brick = pl.program_id(0)

    def samples0(block):
        x = vol0[0, pl.ds(block * 8, 8)].reshape(8 * RC, ROWS)
        return jnp.dot(x, res0[...], preferred_element_type=F32).reshape(8, RC, COLS)

    slot0 = place[2 * brick]
    slot1 = place[2 * brick + 1]

    def write0(c, x):
        out[slot0, c] = x

    def write1(c, x):
        out[slot1, c] = x

    march(samples0, coef, write0)
    half = RC // 2
    for r in range(half):
        x = jnp.concatenate([vol1[0, r], vol1[0, r + half]], axis=0)
        y = lax.dot_general(x, res1[...], (((0,), (0,)), ((), ())), preferred_element_type=F32)
        samples[pl.ds(r, 64, stride=RC), :] = y[:, :COLS]
        samples[pl.ds(r + half, 64, stride=RC), :] = y[:, COLS:]

    def samples1(block):
        return samples[pl.ds(block * 8 * RC, 8 * RC), :].reshape(8, RC, COLS)

    march(samples1, coef, write1)


def render(chunk, place, slope, pivot, res0, res1, volume):
    smem = pl.BlockSpec(memory_space=pltpu.SMEM)
    return pl.pallas_call(
        render_kernel,
        grid=(BRICKS,),
        in_specs=[
            smem,
            smem,
            smem,
            pl.BlockSpec((64, COLS), lambda b: (0, 0)),
            pl.BlockSpec((128, 2 * COLS), lambda b: (0, 0)),
            pl.BlockSpec((1, 64, RC, 64), lambda b: (b, 0, chunk, 0)),
            pl.BlockSpec((1, RC, 64, 64), lambda b: (b, chunk, 0, 0)),
        ],
        out_specs=pl.BlockSpec((SLOTS, 4, RC, COLS), lambda b: (0, 0, 0, 0)),
        out_shape=jax.ShapeDtypeStruct((SLOTS, 4, RC, COLS), BF),
        scratch_shapes=[pltpu.VMEM((64 * RC, COLS), F32)],
        compiler_params=pltpu.CompilerParams(vmem_limit_bytes=32 << 20),
        cost_estimate=pl.CostEstimate(flops=40_000_000_000, bytes_accessed=10_000_000, transcendentals=16_000_000),
        name=f"render{chunk}",
    )(place, slope, pivot, res0, res1, volume, volume)


def compose_kernel(count, order, target, received, out, acc):
    acc[...] = jnp.zeros_like(acc)

    def step(i, _):
        slot = order[i]
        t = target[i]
        x = received[slot].astype(F32)
        inner = acc[t, 3]
        shade = jnp.exp(-inner)
        for c in range(3):
            acc[t, c] = acc[t, c] + x[c] * shade
        acc[t, 3] = inner + x[3]
        return 0

    lax.fori_loop(0, count[0], step, 0)
    out[...] = acc[...].astype(BF)


def compose(chunk, count, order, target, received):
    smem = pl.BlockSpec(memory_space=pltpu.SMEM)
    vmem = pl.BlockSpec(memory_space=pltpu.VMEM)
    return pl.pallas_call(
        compose_kernel,
        in_specs=[smem, smem, smem, vmem],
        out_specs=vmem,
        out_shape=jax.ShapeDtypeStruct((2 * CELLS, 4, RC, COLS), BF),
        scratch_shapes=[pltpu.VMEM((2 * CELLS, 4, RC, COLS), F32)],
        compiler_params=pltpu.CompilerParams(vmem_limit_bytes=32 << 20),
        cost_estimate=pl.CostEstimate(flops=4_000_000, bytes_accessed=1_500_000, transcendentals=200_000),
        name=f"compose{chunk}",
    )(count, order, target, received)


def blend_kernel(chain, *refs):
    bands, (colour, light_out) = refs[:CHUNKS], refs[CHUNKS:]
    for view in range(2):
        for k in range(CHUNKS):
            rows = pl.ds(k * RC, RC)
            front = jnp.zeros((RC, COLS), F32)
            acc = [jnp.zeros((RC, COLS), F32)] * 3
            for j in range(8):
                x = bands[k][chain[view * 8 + j] * 2 + view].astype(F32)
                shade = jnp.exp(-front)
                for c in range(3):
                    acc[c] = acc[c] + shade * x[c]
                front = front + x[3]
            for c in range(3):
                colour[view, c, 0, rows, :] = acc[c]
            light_out[view, 0, rows, :] = jnp.exp(-front)


def blend(chain, bands):
    smem = pl.BlockSpec(memory_space=pltpu.SMEM)
    vmem = pl.BlockSpec(memory_space=pltpu.VMEM)
    return pl.pallas_call(
        blend_kernel,
        in_specs=[smem] + [vmem] * CHUNKS,
        out_specs=[vmem, vmem],
        out_shape=[
            jax.ShapeDtypeStruct((2, 3, 1, ROWS, COLS), F32),
            jax.ShapeDtypeStruct((2, 1, ROWS, COLS), F32),
        ],
        compiler_params=pltpu.CompilerParams(vmem_limit_bytes=32 << 20),
        name="blend",
    )(chain, *bands)


def body(volume, resampler, slope, pivot, tile_owner, tile_cell, depth_order, slab_rank):
    ids = jnp.arange(32)
    owner = tile_owner.reshape(-1)
    same = (owner[None, :] == owner[:, None]) & (ids[None, :] < ids[:, None])
    place = owner * 2 + jnp.sum(same.astype(jnp.int32), axis=1)
    view = jnp.tile(jnp.arange(2, dtype=jnp.int32), BRICKS)
    tag = depth_order.T.reshape(-1) * 16 + tile_cell.reshape(-1) * 2 + view
    hit = place[None, :] == jnp.arange(SLOTS, dtype=jnp.int32)[:, None]
    empty = 1 << 20
    slot_tag = jnp.min(jnp.where(hit, tag[None, :], empty), axis=1)
    tags = lax.all_to_all(slot_tag.reshape(OWNERS, 2), "tile", split_axis=0, concat_axis=0, tiled=True).reshape(-1)
    filled = tags < empty
    slots = jnp.arange(SLOTS, dtype=jnp.int32)
    before = (tags[None, :] < tags[:, None]) | ((tags[None, :] == tags[:, None]) & (slots[None, :] < slots[:, None]))
    position = jnp.sum(before.astype(jnp.int32), axis=1)
    at = position[None, :] == slots[:, None]
    order = jnp.sum(jnp.where(at, slots[None, :], 0), axis=1)
    target = jnp.sum(jnp.where(at, jnp.where(filled, tags % 16, 0)[None, :], 0), axis=1)
    count = jnp.sum(filled.astype(jnp.int32)).reshape(1)
    slabs = jnp.arange(8, dtype=jnp.int32)
    chain = jnp.sum(
        jnp.where(slab_rank[:, None, :] == slabs[None, :, None], slabs[None, None, :], 0), axis=2
    ).reshape(-1)
    res0 = resampler[0]
    zero = jnp.zeros_like(res0)
    res1 = jnp.concatenate(
        [jnp.concatenate([resampler[1], zero], 1), jnp.concatenate([zero, resampler[1]], 1)], 0
    )
    bands = []
    for k in range(CHUNKS):
        sent = render(k, place, slope, pivot, res0, res1, volume)
        got = lax.all_to_all(sent.reshape(OWNERS, 2, 4, RC, COLS), "tile", split_axis=0, concat_axis=0, tiled=True)
        piece = compose(k, count, order, target, got.reshape(SLOTS, 4, RC, COLS))
        bands.append(
            lax.all_to_all(piece.reshape(8, 2, 4, RC, COLS), "depth", split_axis=0, concat_axis=0, tiled=True).reshape(
                16, 4, RC, COLS
            )
        )
    return tuple(blend(chain, bands))


def solution(mesh):
    in_specs = (
        P(("depth", "tile"), None, None, None),
        P(),
        P(),
        P(),
        P(("depth", "tile"), None),
        P(("depth", "tile"), None),
        P(None, ("depth", "tile")),
        P(),
    )
    out_specs = (P(None, None, "tile", "depth", None), P(None, "tile", "depth", None))
    return jax.shard_map(body, mesh=mesh, in_specs=in_specs, out_specs=out_specs, check_vma=False)
```

time: 645 us -> 221 us (0.34); the launches traced: 635 us -> 218 us
  other arithmetic: 176 us -> 2.75 us
  waiting for transfers between devices: 180 us -> 39.7 us
  matrix products: 125 us -> 0 us
  Pallas kernels: 0 us -> 79.3 us
  local copies, waits for them, and re-layouts: 108 us -> 29.5 us
  starting transfers between devices: 20.2 us -> 66.4 us
  blocking collectives: 24.7 us -> 0 us
    reduce_sum x19 -> x4, other arithmetic: 149 us -> 0.61 us  [the longest x1 0.18 us: body(): position = jnp.sum(before.astype(jnp.int32), axis=1)]
    all_to_all x2 -> x9, waiting for transfers between devices: 180 us -> 39.7 us  [the longest x4 22.8 us: body(): lax.all_to_all(sent.reshape(OWNERS, 2, 4, RC, COLS), 'tile', split_axis=0...]
    dot_general x52 -> x0, matrix products: 125 us -> none  [the longest x16 106 us: render_brick(): jnp.einsum('kj,vjrs->vkrs', strict_lower, optical, precision=TOP_PRECISION)]
    pallas_call x0 -> x9, Pallas kernels: none -> 79.3 us  [the longest x4 66 us: render(): pl.pallas_call(render_kernel, grid=(BRICKS,), in_specs=[smem, smem, smem,...]
    all_to_all x2 -> x9, starting transfers between devices: 20.2 us -> 66.4 us  [the longest x4 32.5 us: body(): lax.all_to_all(sent.reshape(OWNERS, 2, 4, RC, COLS), 'tile', split_axis=0...]
    squeeze x32 -> x1, local copies, waits for them, and re-layouts: 46.6 us -> 0.74 us  [body(): resampler[1]]
    unnamed x5 -> x23, local copies, waits for them, and re-layouts: 2.22 us -> 27.1 us
    slice x19 -> x0, local copies, waits for them, and re-layouts: 24.9 us -> none  [the longest x16 23.2 us: render_brick(): ramp_slope[channel] * (samples - ramp_pivot[channel])]
  transfers between devices with their start and end apart: 2 -> 9, of which waited for: 1 -> 8; matrix products, arithmetic and copies ran while one was open for 59% -> 1% of each run, Pallas kernels for 0% -> 36%
where the time goes in v1:
time: 221 us; the launch traced here: 218 us
  Pallas kernels  79.3 us (36%)
  starting transfers between devices  66.4 us (30%)
  waiting for transfers between devices  39.7 us (18%)
  local copies, waits for them, and re-layouts  29.5 us (13%)
  other arithmetic  2.75 us (1%)
    pallas_call x4, Pallas kernels, render(): pl.pallas_call(render_kernel, grid=(BRICKS,), in_specs=[smem, smem, smem,...  66 us
    all_to_all x4, starting transfers between devices, body(): lax.all_to_all(sent.reshape(OWNERS, 2, 4, RC, COLS), 'tile', split_axis=0...  32.5 us
    unnamed x23, local copies, waits for them, and re-layouts  27.1 us
    all_to_all x4, starting transfers between devices, body(): lax.all_to_all(piece.reshape(8, 2, 4, RC, COLS), 'depth', split_axis=0, c...  23.1 us
    all_to_all x4, waiting for transfers between devices, body(): lax.all_to_all(sent.reshape(OWNERS, 2, 4, RC, COLS), 'tile', split_axis=0...  22.8 us
    all_to_all x4, waiting for transfers between devices, body(): lax.all_to_all(piece.reshape(8, 2, 4, RC, COLS), 'depth', split_axis=0, c...  16.8 us
    pallas_call x4, Pallas kernels, compose(): pl.pallas_call(compose_kernel, in_specs=[smem, smem, smem, vmem], out_spe...  11.8 us
    all_to_all x1, starting transfers between devices, body(): lax.all_to_all(slot_tag.reshape(OWNERS, 2), 'tile', split_axis=0, concat_...  10.8 us
  transfers between devices with their start and end apart: 9, of which 8 were waited for; matrix products, arithmetic and copies ran while one was open for 1% of the time, Pallas kernels for 36%

profile of v1, /device:TPU:33, one launch (start us, length us, event | category | flops | bytes accessed | tf_op | source)
XLA Modules:
  0.0 218.4 jit_solution(11132869615603320268)
XLA Ops:
  0.6 0.8 copy.17
  1.4 0.1 reshape.141
  1.5 0.2 convert_reduce_fusion.1
  1.7 0.7 fusion.7
  2.5 0.1 add.38
  2.5 0.1 select_reduce_fusion.2
  2.6 0.7 all_to_all.30
  3.4 10.8 %all-to-all-start = ((s32[32,1,2]{2,1,0:T(1,128)}), s32[32,1,2]{2,1,0:T(1,128)S(1)}, u32[]{:S(2)}, u32[]{:S(2)}) async-start(s32[32,1,2]{2,1,0:T(1,128)} %bitcast.1), calls=%async_computation | async-start | bytes 32768 | tf_op jit(solution)/shard_map/all_to_all | solution.py:179
  14.2 0.7 slice_bitcast_fusion
  14.9 5.8 %copy-done.2 = bf16[16,64,64,64]{3,2,1,0:T(8,128)(2,1)S(1)} copy-done((bf16[16,64,64,64]{3,2,1,0:T(8,128)(2,1)S(1)}, bf16[16,64,64,64]{3,2,1,0:T(8,128)(2,1)}, u32[]{:S(2)}) %copy-start.2) | copy-done | bytes 8388632
  20.7 0.7 copy-done.6
  21.4 0.7 copy-done.8
  22.0 17.0 %render1.1 = bf16[64,4,16,128]{3,2,1,0:T(8,128)(2,1)} custom-call(s32[32]{0:T(128)S(1)} %multiply_add_fusion.place, f32[3]{0:T(128)S(1)} %copy-done.6, f32[3]{0:T(128)S(1)} %copy-done.8, bf16[64,128]{1,0:T(8,128)(2,1)S(1)} %get-tuple-element.7.res0, bf16[128,256]{1,0:T(8,128)(2,1)S(1)} %fusion.2.res1, bf16[16,64,64,64]{3,2,1,0:T(8,128)(2,1)S(1)} %copy-done.2, ...), custom_call_target="tpu_custom_call" | custom-call | flops 40000000000 | bytes 10000000 | tf_op jit(solution)/shard_map/render1/pallas_call | solution.py:81
  39.0 9.2 %all-to-all-start.3 = ((bf16[32,2,4,16,128]{4,3,2,1,0:T(8,128)(2,1)}), bf16[32,2,4,16,128]{4,3,2,1,0:T(8,128)(2,1)S(1)}, u32[]{:S(2)}, u32[]{:S(2)}) async-start(bf16[32,2,4,16,128]{4,3,2,1,0:T(8,128)(2,1)} %bitcast.9), calls=%async_computation.3 | async-start | bytes 2097152 | tf_op jit(solution)/shard_map/all_to_all | solution.py:200
  48.3 5.8 %copy-done.3 = bf16[16,64,64,64]{3,2,1,0:T(8,128)(2,1)S(1)} copy-done((bf16[16,64,64,64]{3,2,1,0:T(8,128)(2,1)S(1)}, bf16[16,64,64,64]{3,2,1,0:T(8,128)(2,1)}, u32[]{:S(2)}) %copy-start.3) | copy-done | bytes 8388632
  54.1 17.0 %render2.1 = bf16[64,4,16,128]{3,2,1,0:T(8,128)(2,1)} custom-call(s32[32]{0:T(128)S(1)} %multiply_add_fusion.place, f32[3]{0:T(128)S(1)} %copy-done.7, f32[3]{0:T(128)S(1)} %copy-done.9, bf16[64,128]{1,0:T(8,128)(2,1)S(1)} %get-tuple-element.7.res0, bf16[128,256]{1,0:T(8,128)(2,1)S(1)} %fusion.2.res1, bf16[16,64,64,64]{3,2,1,0:T(8,128)(2,1)S(1)} %copy-done.3, ...), custom_call_target="tpu_custom_call" | custom-call | flops 40000000000 | bytes 10000000 | tf_op jit(solution)/shard_map/render2/pallas_call | solution.py:81
  71.0 2.0 all-to-all-done.3
  73.0 7.6 %all-to-all-start.5 = ((bf16[32,2,4,16,128]{4,3,2,1,0:T(8,128)(2,1)}), bf16[32,2,4,16,128]{4,3,2,1,0:T(8,128)(2,1)S(1)}, u32[]{:S(2)}, u32[]{:S(2)}) async-start(bf16[32,2,4,16,128]{4,3,2,1,0:T(8,128)(2,1)} %bitcast.13), calls=%async_computation.5 | async-start | bytes 2097152 | tf_op jit(solution)/shard_map/all_to_all | solution.py:200
  80.6 5.8 %copy-done.4 = bf16[16,64,64,64]{3,2,1,0:T(8,128)(2,1)S(1)} copy-done((bf16[16,64,64,64]{3,2,1,0:T(8,128)(2,1)S(1)}, bf16[16,64,64,64]{3,2,1,0:T(8,128)(2,1)}, u32[]{:S(2)}) %copy-start.4) | copy-done | bytes 8388632
  86.3 16.0 %render3.1 = bf16[64,4,16,128]{3,2,1,0:T(8,128)(2,1)S(1)} custom-call(s32[32]{0:T(128)S(1)} %multiply_add_fusion.place, f32[3]{0:T(128)S(1)} %copy-done.7, f32[3]{0:T(128)S(1)} %copy-done.9, bf16[64,128]{1,0:T(8,128)(2,1)S(1)} %get-tuple-element.7.res0, bf16[128,256]{1,0:T(8,128)(2,1)S(1)} %fusion.2.res1, bf16[16,64,64,64]{3,2,1,0:T(8,128)(2,1)S(1)} %copy-done.4, ...), custom_call_target="tpu_custom_call" | custom-call | flops 40000000000 | bytes 10000000 | tf_op jit(solution)/shard_map/render3/pallas_call | solution.py:81
  102.4 1.0 copy-done.1
  103.4 1.4 all-to-all-done.5
  104.8 7.8 %all-to-all-start.7 = ((bf16[32,2,4,16,128]{4,3,2,1,0:T(8,128)(2,1)}), bf16[32,2,4,16,128]{4,3,2,1,0:T(8,128)(2,1)S(1)}, u32[]{:S(2)}, u32[]{:S(2)}) async-start(bf16[32,2,4,16,128]{4,3,2,1,0:T(8,128)(2,1)} %bitcast.30), calls=%async_computation.7 | async-start | bytes 2097152 | tf_op jit(solution)/shard_map/all_to_all | solution.py:200
  112.6 5.8 %copy-done.5 = bf16[16,64,64,64]{3,2,1,0:T(8,128)(2,1)S(1)} copy-done((bf16[16,64,64,64]{3,2,1,0:T(8,128)(2,1)S(1)}, bf16[16,64,64,64]{3,2,1,0:T(8,128)(2,1)}, u32[]{:S(2)}) %copy-start.5) | copy-done | bytes 8388632
  118.4 16.0 %render0.1 = bf16[64,4,16,128]{3,2,1,0:T(8,128)(2,1)S(1)} custom-call(s32[32]{0:T(128)S(1)} %multiply_add_fusion.place, f32[3]{0:T(128)S(1)} %copy-done.7, f32[3]{0:T(128)S(1)} %copy-done.9, bf16[64,128]{1,0:T(8,128)(2,1)S(1)} %get-tuple-element.7.res0, bf16[128,256]{1,0:T(8,128)(2,1)S(1)} %fusion.2.res1, bf16[16,64,64,64]{3,2,1,0:T(8,128)(2,1)S(1)} %copy-done.5, ...), custom_call_target="tpu_custom_call" | custom-call | flops 40000000000 | bytes 10000000 | tf_op jit(solution)/shard_map/render0/pallas_call | solution.py:81
  134.4 1.0 copy-done
  135.4 1.3 all-to-all-done.7
  136.7 8.0 %all-to-all-start.1 = ((bf16[32,2,4,16,128]{4,3,2,1,0:T(8,128)(2,1)}), bf16[32,2,4,16,128]{4,3,2,1,0:T(8,128)(2,1)}, u32[]{:S(2)}, u32[]{:S(2)}) async-start(bf16[32,2,4,16,128]{4,3,2,1,0:T(8,128)(2,1)} %bitcast.29), calls=%async_computation.1 | async-start | bytes 2097152 | tf_op jit(solution)/shard_map/all_to_all | solution.py:200
  144.7 0.5 broadcast.80
  145.2 1.3 fusion.9
  146.5 0.1 lt.72
  146.6 0.2 convert_reduce_fusion
  146.8 0.1 select_reduce_fusion
  147.0 2.8 %compose1.1 = bf16[16,4,16,128]{3,2,1,0:T(8,128)(2,1)} custom-call(s32[1]{0:T(128)} %bitcast.2.count, s32[64]{0:T(128)S(1)} %get-tuple-element.5.order, s32[64]{0:T(128)S(1)} %get-tuple-element.4.target, bf16[64,4,16,128]{3,2,1,0:T(8,128)(2,1)S(1)} %bitcast.28), custom_call_target="tpu_custom_call" | custom-call | flops 4000000 | bytes 1500000 | tf_op jit(solution)/shard_map/compose1/pallas_call | solution.py:123
  149.7 18.1 %all-to-all-done.1 = bf16[32,2,4,16,128]{4,3,2,1,0:T(8,128)(2,1)} async-done(((bf16[32,2,4,16,128]{4,3,2,1,0:T(8,128)(2,1)}), bf16[32,2,4,16,128]{4,3,2,1,0:T(8,128)(2,1)}, u32[]{:S(2)}, u32[]{:S(2)}) %all-to-all-start.1) | async-done | bytes 1048608 | tf_op jit(solution)/shard_map/all_to_all | solution.py:200
  167.8 10.0 %all-to-all-start.4 = ((bf16[8,2,4,16,128]{4,3,2,1,0:T(8,128)(2,1)}), bf16[8,2,4,16,128]{4,3,2,1,0:T(8,128)(2,1)S(1)}, u32[]{:S(2)}, u32[]{:S(2)}) async-start(bf16[8,2,4,16,128]{4,3,2,1,0:T(8,128)(2,1)} %bitcast.11), calls=%async_computation.4 | async-start | bytes 524288 | tf_op jit(solution)/shard_map/all_to_all | solution.py:203
  177.8 2.8 %compose2.1 = bf16[16,4,16,128]{3,2,1,0:T(8,128)(2,1)} custom-call(s32[1]{0:T(128)} %bitcast.2.count, s32[64]{0:T(128)S(1)} %get-tuple-element.5.order, s32[64]{0:T(128)S(1)} %get-tuple-element.4.target, bf16[64,4,16,128]{3,2,1,0:T(8,128)(2,1)S(1)} %bitcast.27), custom_call_target="tpu_custom_call" | custom-call | flops 4000000 | bytes 1500000 | tf_op jit(solution)/shard_map/compose2/pallas_call | solution.py:123
  180.6 3.7 %all-to-all-done.4 = bf16[8,2,4,16,128]{4,3,2,1,0:T(8,128)(2,1)S(1)} async-done(((bf16[8,2,4,16,128]{4,3,2,1,0:T(8,128)(2,1)}), bf16[8,2,4,16,128]{4,3,2,1,0:T(8,128)(2,1)S(1)}, u32[]{:S(2)}, u32[]{:S(2)}) %all-to-all-start.4) | async-done | bytes 262176 | tf_op jit(solution)/shard_map/all_to_all | solution.py:203
  184.3 4.4 %all-to-all-start.6 = ((bf16[8,2,4,16,128]{4,3,2,1,0:T(8,128)(2,1)}), bf16[8,2,4,16,128]{4,3,2,1,0:T(8,128)(2,1)S(1)}, u32[]{:S(2)}, u32[]{:S(2)}) async-start(bf16[8,2,4,16,128]{4,3,2,1,0:T(8,128)(2,1)} %bitcast.15), calls=%async_computation.6 | async-start | bytes 524288 | tf_op jit(solution)/shard_map/all_to_all | solution.py:203
  188.7 2.8 %compose3.1 = bf16[16,4,16,128]{3,2,1,0:T(8,128)(2,1)} custom-call(s32[1]{0:T(128)} %bitcast.2.count, s32[64]{0:T(128)S(1)} %get-tuple-element.5.order, s32[64]{0:T(128)S(1)} %get-tuple-element.4.target, bf16[64,4,16,128]{3,2,1,0:T(8,128)(2,1)S(1)} %bitcast.26), custom_call_target="tpu_custom_call" | custom-call | flops 4000000 | bytes 1500000 | tf_op jit(solution)/shard_map/compose3/pallas_call | solution.py:123
  191.5 3.7 %all-to-all-done.6 = bf16[8,2,4,16,128]{4,3,2,1,0:T(8,128)(2,1)S(1)} async-done(((bf16[8,2,4,16,128]{4,3,2,1,0:T(8,128)(2,1)}), bf16[8,2,4,16,128]{4,3,2,1,0:T(8,128)(2,1)S(1)}, u32[]{:S(2)}, u32[]{:S(2)}) %all-to-all-start.6) | async-done | bytes 262176 | tf_op jit(solution)/shard_map/all_to_all | solution.py:203
  195.2 4.4 %all-to-all-start.8 = ((bf16[8,2,4,16,128]{4,3,2,1,0:T(8,128)(2,1)}), bf16[8,2,4,16,128]{4,3,2,1,0:T(8,128)(2,1)S(1)}, u32[]{:S(2)}, u32[]{:S(2)}) async-start(bf16[8,2,4,16,128]{4,3,2,1,0:T(8,128)(2,1)} %bitcast.19), calls=%async_computation.8 | async-start | bytes 524288 | tf_op jit(solution)/shard_map/all_to_all | solution.py:203
  199.6 3.5 %compose0.1 = bf16[16,4,16,128]{3,2,1,0:T(8,128)(2,1)} custom-call(s32[1]{0:T(128)} %bitcast.2.count, s32[64]{0:T(128)S(1)} %get-tuple-element.5.order, s32[64]{0:T(128)S(1)} %get-tuple-element.4.target, bf16[64,4,16,128]{3,2,1,0:T(8,128)(2,1)} %bitcast.6.received), custom_call_target="tpu_custom_call" | custom-call | flops 4000000 | bytes 1500000 | tf_op jit(solution)/shard_map/compose0/pallas_call | solution.py:123
  203.0 3.1 %all-to-all-done.8 = bf16[8,2,4,16,128]{4,3,2,1,0:T(8,128)(2,1)S(1)} async-done(((bf16[8,2,4,16,128]{4,3,2,1,0:T(8,128)(2,1)}), bf16[8,2,4,16,128]{4,3,2,1,0:T(8,128)(2,1)S(1)}, u32[]{:S(2)}, u32[]{:S(2)}) %all-to-all-start.8) | async-done | bytes 262176 | tf_op jit(solution)/shard_map/all_to_all | solution.py:203
  206.1 4.4 %all-to-all-start.2 = ((bf16[8,2,4,16,128]{4,3,2,1,0:T(8,128)(2,1)}), bf16[8,2,4,16,128]{4,3,2,1,0:T(8,128)(2,1)S(1)}, u32[]{:S(2)}, u32[]{:S(2)}) async-start(bf16[8,2,4,16,128]{4,3,2,1,0:T(8,128)(2,1)} %bitcast.7), calls=%async_computation.2 | async-start | bytes 524288 | tf_op jit(solution)/shard_map/all_to_all | solution.py:203
  210.4 0.1 select_reduce_fusion.3
  210.7 6.3 %all-to-all-done.2 = bf16[8,2,4,16,128]{4,3,2,1,0:T(8,128)(2,1)S(1)} async-done(((bf16[8,2,4,16,128]{4,3,2,1,0:T(8,128)(2,1)}), bf16[8,2,4,16,128]{4,3,2,1,0:T(8,128)(2,1)S(1)}, u32[]{:S(2)}, u32[]{:S(2)}) %all-to-all-start.2) | async-done | bytes 262176 | tf_op jit(solution)/shard_map/all_to_all | solution.py:203
  217.0 1.5 blend.1
  (20 shorter events, 0.2 us)
Async XLA Ops:
  3.4 35.7 %all-to-all-start = ((s32[32,1,2]{2,1,0:T(1,128)}), s32[32,1,2]{2,1,0:T(1,128)S(1)}, u32[]{:S(2)}, u32[]{:S(2)}) async-start(s32[32,1,2]{2,1,0:T(1,128)} %bitcast.1), calls=%async_computation | async-start | bytes 32768 | tf_op jit(solution)/shard_map/all_to_all | solution.py:179
  14.9 5.8 %copy-start.2 = (bf16[16,64,64,64]{3,2,1,0:T(8,128)(2,1)S(1)}, bf16[16,64,64,64]{3,2,1,0:T(8,128)(2,1)}, u32[]{:S(2)}) copy-start(bf16[16,64,64,64]{3,2,1,0:T(8,128)(2,1)} %vol1.7) | copy-start | bytes 25165828
  20.7 0.7 copy-start.6
  21.3 0.7 copy-start.8
  22.0 26.3 %copy-start.7 = (f32[3]{0:T(128)S(1)}, f32[3]{0:T(128)}, u32[]{:S(2)}) copy-start(f32[3]{0:T(128)} %slope.7) | copy-start | bytes 40
  22.0 26.3 %copy-start.9 = (f32[3]{0:T(128)S(1)}, f32[3]{0:T(128)}, u32[]{:S(2)}) copy-start(f32[3]{0:T(128)} %pivot.7) | copy-start | bytes 40
  39.0 34.0 %all-to-all-start.3 = ((bf16[32,2,4,16,128]{4,3,2,1,0:T(8,128)(2,1)}), bf16[32,2,4,16,128]{4,3,2,1,0:T(8,128)(2,1)S(1)}, u32[]{:S(2)}, u32[]{:S(2)}) async-start(bf16[32,2,4,16,128]{4,3,2,1,0:T(8,128)(2,1)} %bitcast.9), calls=%async_computation.3 | async-start | bytes 2097152 | tf_op jit(solution)/shard_map/all_to_all | solution.py:200
  48.3 5.8 %copy-start.3 = (bf16[16,64,64,64]{3,2,1,0:T(8,128)(2,1)S(1)}, bf16[16,64,64,64]{3,2,1,0:T(8,128)(2,1)}, u32[]{:S(2)}) copy-start(bf16[16,64,64,64]{3,2,1,0:T(8,128)(2,1)} %vol1.7) | copy-start | bytes 25165828
  73.0 31.8 %all-to-all-start.5 = ((bf16[32,2,4,16,128]{4,3,2,1,0:T(8,128)(2,1)}), bf16[32,2,4,16,128]{4,3,2,1,0:T(8,128)(2,1)S(1)}, u32[]{:S(2)}, u32[]{:S(2)}) async-start(bf16[32,2,4,16,128]{4,3,2,1,0:T(8,128)(2,1)} %bitcast.13), calls=%async_computation.5 | async-start | bytes 2097152 | tf_op jit(solution)/shard_map/all_to_all | solution.py:200
  80.6 5.8 %copy-start.4 = (bf16[16,64,64,64]{3,2,1,0:T(8,128)(2,1)S(1)}, bf16[16,64,64,64]{3,2,1,0:T(8,128)(2,1)}, u32[]{:S(2)}) copy-start(bf16[16,64,64,64]{3,2,1,0:T(8,128)(2,1)} %vol1.7) | copy-start | bytes 25165828
  102.4 1.0 copy-start.1
  104.8 31.9 %all-to-all-start.7 = ((bf16[32,2,4,16,128]{4,3,2,1,0:T(8,128)(2,1)}), bf16[32,2,4,16,128]{4,3,2,1,0:T(8,128)(2,1)S(1)}, u32[]{:S(2)}, u32[]{:S(2)}) async-start(bf16[32,2,4,16,128]{4,3,2,1,0:T(8,128)(2,1)} %bitcast.30), calls=%async_computation.7 | async-start | bytes 2097152 | tf_op jit(solution)/shard_map/all_to_all | solution.py:200
  112.6 5.8 %copy-start.5 = (bf16[16,64,64,64]{3,2,1,0:T(8,128)(2,1)S(1)}, bf16[16,64,64,64]{3,2,1,0:T(8,128)(2,1)}, u32[]{:S(2)}) copy-start(bf16[16,64,64,64]{3,2,1,0:T(8,128)(2,1)} %vol1.7) | copy-start | bytes 25165828
  118.4 92.1 %copy-start.10 = (s32[2,8]{1,0:T(2,128)S(1)}, s32[2,8]{1,0:T(2,128)}, u32[]{:S(2)}) copy-start(s32[2,8]{1,0:T(2,128)} %param.15) | copy-start | bytes 196
  134.4 1.0 copy-start
  136.7 31.1 %all-to-all-start.1 = ((bf16[32,2,4,16,128]{4,3,2,1,0:T(8,128)(2,1)}), bf16[32,2,4,16,128]{4,3,2,1,0:T(8,128)(2,1)}, u32[]{:S(2)}, u32[]{:S(2)}) async-start(bf16[32,2,4,16,128]{4,3,2,1,0:T(8,128)(2,1)} %bitcast.29), calls=%async_computation.1 | async-start | bytes 2097152 | tf_op jit(solution)/shard_map/all_to_all | solution.py:200
  167.8 16.5 %all-to-all-start.4 = ((bf16[8,2,4,16,128]{4,3,2,1,0:T(8,128)(2,1)}), bf16[8,2,4,16,128]{4,3,2,1,0:T(8,128)(2,1)S(1)}, u32[]{:S(2)}, u32[]{:S(2)}) async-start(bf16[8,2,4,16,128]{4,3,2,1,0:T(8,128)(2,1)} %bitcast.11), calls=%async_computation.4 | async-start | bytes 524288 | tf_op jit(solution)/shard_map/all_to_all | solution.py:203
  184.3 10.9 %all-to-all-start.6 = ((bf16[8,2,4,16,128]{4,3,2,1,0:T(8,128)(2,1)}), bf16[8,2,4,16,128]{4,3,2,1,0:T(8,128)(2,1)S(1)}, u32[]{:S(2)}, u32[]{:S(2)}) async-start(bf16[8,2,4,16,128]{4,3,2,1,0:T(8,128)(2,1)} %bitcast.15), calls=%async_computation.6 | async-start | bytes 524288 | tf_op jit(solution)/shard_map/all_to_all | solution.py:203
  195.2 10.9 %all-to-all-start.8 = ((bf16[8,2,4,16,128]{4,3,2,1,0:T(8,128)(2,1)}), bf16[8,2,4,16,128]{4,3,2,1,0:T(8,128)(2,1)S(1)}, u32[]{:S(2)}, u32[]{:S(2)}) async-start(bf16[8,2,4,16,128]{4,3,2,1,0:T(8,128)(2,1)} %bitcast.19), calls=%async_computation.8 | async-start | bytes 524288 | tf_op jit(solution)/shard_map/all_to_all | solution.py:203
  206.1 10.9 %all-to-all-start.2 = ((bf16[8,2,4,16,128]{4,3,2,1,0:T(8,128)(2,1)}), bf16[8,2,4,16,128]{4,3,2,1,0:T(8,128)(2,1)S(1)}, u32[]{:S(2)}, u32[]{:S(2)}) async-start(bf16[8,2,4,16,128]{4,3,2,1,0:T(8,128)(2,1)} %bitcast.7), calls=%async_computation.2 | async-start | bytes 524288 | tf_op jit(solution)/shard_map/all_to_all | solution.py:203

commit v2 on v1

v2 whole, which is shorter than its diff:
```python
import jax
import jax.numpy as jnp
from jax import lax
from jax.experimental import pallas as pl
from jax.experimental.pallas import tpu as pltpu
from jax.sharding import PartitionSpec as P

BF = jnp.bfloat16
F32 = jnp.float32
I32 = jnp.int32
MESH = pl.DeviceIdType.MESH
ROWS = 64
COLS = 128
BRICKS = 16
ITEMS = 2 * BRICKS
NZ, NY = 8, 4
OWNERS = NZ * NY
SLABS = 8
SLOTS = 64
TARGETS = 16
RC = 16
CHUNKS = ROWS // RC
EMPTY = 1 << 20
EXP_SCALE = -1.4426950408889634 / 64.0


def march(samples_of, coef, write):
    zero = jnp.zeros((RC, COLS), F32)

    def step(block, carry):
        front, light, a0, a1, a2 = carry
        acc = [a0, a1, a2]
        rows = samples_of(block)
        for j in range(8):
            s = rows[j]
            front = front + s
            after = jnp.exp2(front * EXP_SCALE)
            weight = light - after
            light = after
            for c in range(3):
                acc[c] = acc[c] + weight * jnp.tanh(s * coef[c][0] + coef[c][1])
        return (front, light, *acc)

    front, light, a0, a1, a2 = lax.fori_loop(0, 8, step, (zero, zero + 1.0, zero, zero, zero), unroll=8)
    total = 1.0 - light
    for c, acc in enumerate((a0, a1, a2)):
        write(c, (0.5 * (total + acc)).astype(BF))
    write(3, (front * (1.0 / 64.0)).astype(BF))


def render_rows(brick, chunk, coef, res0, res1, bricks, samples, prints):
    top = pl.multiple_of(chunk * RC, RC)

    def samples0(block):
        x = bricks[brick, pl.ds(block * 8, 8), pl.ds(top, RC), :].reshape(8 * RC, ROWS)
        return jnp.dot(x, res0[...], preferred_element_type=F32).reshape(8, RC, COLS)

    def write0(c, x):
        prints[2 * brick, c] = x

    march(samples0, coef, write0)
    half = RC // 2
    for r in range(half):
        x = jnp.concatenate([bricks[brick, top + r], bricks[brick, top + r + half]], axis=0)
        y = lax.dot_general(x, res1[...], (((0,), (0,)), ((), ())), preferred_element_type=F32)
        samples[pl.ds(r, 64, stride=RC), :] = y[:, :COLS]
        samples[pl.ds(r + half, 64, stride=RC), :] = y[:, COLS:]

    def samples1(block):
        return samples[pl.ds(block * 8 * RC, 8 * RC), :].reshape(8, RC, COLS)

    def write1(c, x):
        prints[2 * brick + 1, c] = x

    march(samples1, coef, write1)


def depth_table(tag_land, table):
    tags = tag_land[:, 0, :]
    col = jnp.concatenate([tags[:, 0:1], tags[:, 1:2]], axis=0)
    sub = lax.broadcasted_iota(I32, (SLOTS, SLOTS), 0)
    lane = lax.broadcasted_iota(I32, (SLOTS, SLOTS), 1)
    key_col = jnp.broadcast_to(col, (SLOTS, SLOTS)) * SLOTS + sub
    key_row = jnp.broadcast_to(jnp.sum(jnp.where(sub == lane, key_col, 0), axis=0, keepdims=True), (SLOTS, SLOTS))
    place_col = jnp.broadcast_to(
        jnp.sum(jnp.where(key_row < key_col, 1, 0), axis=1, keepdims=True), (SLOTS, SLOTS)
    )
    slot_col = (sub % OWNERS) * 2 + sub // OWNERS
    order = jnp.sum(jnp.where(place_col == lane, slot_col, 0), axis=0, keepdims=True)
    sorted_row = jnp.broadcast_to(
        jnp.sum(jnp.where(place_col == lane, key_col, 0), axis=0, keepdims=True), (SLOTS, SLOTS)
    )
    place_row = jnp.broadcast_to(
        jnp.sum(jnp.where(sub == lane, place_col, 0), axis=0, keepdims=True), (SLOTS, SLOTS)
    )
    sorted_col = jnp.broadcast_to(
        jnp.sum(jnp.where(place_row == sub, key_row, 0), axis=1, keepdims=True), (SLOTS, SLOTS)
    )
    target_row = (sorted_row // SLOTS) % TARGETS
    target_col = (sorted_col // SLOTS) % TARGETS
    mate = (target_row == target_col) & (sub < lane)
    prev = jnp.max(jnp.where(mate, sub, -1), axis=0, keepdims=True)
    prev = jnp.where(prev < 0, SLOTS, prev)
    mine = (target_col == lane) & (sorted_col < EMPTY * SLOTS)
    last = jnp.max(jnp.where(mine, sub, -1), axis=0, keepdims=True)
    last = jnp.where(last < 0, SLOTS, last)
    table[0:1, 0:SLOTS] = order
    table[1:2, 0:SLOTS] = prev
    table[2:3, 0:SLOTS] = last


def kernel(
    item_of, chain, slope, pivot, tag_send, res0, res1, volume,
    colour, light_out,
    bricks, prints, samples, stage, landed, local, run, pieces, bands, band, tag_land, table, table_s,
    vol_sem, send_sem, recv_sem, out_sem, in_sem, tag_out, tag_in, table_sem,
):
    slab = lax.axis_index("depth")
    tile = lax.axis_index("tile")
    z, y = tile // NY, tile % NY

    def hop(j):
        m = j // NY
        return (2 * (m % 2) - 1) * ((m + 1) // 2), j % NY

    def peer(j):
        dz, dy = hop(j)
        return ((z + dz + NZ) % NZ) * NY + (y + dy) % NY

    def source(j):
        dz, dy = hop(j)
        return ((z - dz + NZ) % NZ) * NY + (y - dy + NY) % NY

    def brick_copy(b):
        return pltpu.make_async_copy(volume.at[b], bricks.at[b], vol_sem.at[b])

    def tile_copy(chunk, j, land):
        return pltpu.make_async_remote_copy(
            src_ref=stage.at[chunk, pl.ds(2 * peer(j), 2)],
            dst_ref=landed.at[chunk, pl.ds(2 * land, 2)],
            send_sem=send_sem.at[chunk, j],
            recv_sem=recv_sem.at[chunk, j],
            device_id={"tile": peer(j)},
            device_id_type=MESH,
        )

    def tag_copy(j, land):
        return pltpu.make_async_remote_copy(
            src_ref=tag_send.at[peer(j)],
            dst_ref=tag_land.at[land],
            send_sem=tag_out.at[j],
            recv_sem=tag_in.at[j],
            device_id={"tile": peer(j)},
            device_id_type=MESH,
        )

    def slab_copy(chunk, e, land):
        there = (slab + e) % SLABS
        return pltpu.make_async_remote_copy(
            src_ref=pieces.at[chunk, pl.ds(2 * there, 2)],
            dst_ref=bands.at[chunk, pl.ds(2 * land, 2)],
            send_sem=out_sem.at[chunk, e],
            recv_sem=in_sem.at[chunk, e],
            device_id={"depth": there},
            device_id_type=MESH,
        )

    def each(low, high, do):
        def step(i, _):
            do(i)
            return 0

        lax.fori_loop(low, high, step, 0)

    each(0, BRICKS, lambda b: brick_copy(b).start())
    barrier = pltpu.get_barrier_semaphore()
    each(
        1,
        OWNERS,
        lambda j: pl.semaphore_signal(barrier, inc=1, device_id={"tile": peer(j)}, device_id_type=MESH),
    )
    each(
        1,
        SLABS,
        lambda e: pl.semaphore_signal(
            barrier, inc=1, device_id={"depth": (slab + e) % SLABS}, device_id_type=MESH
        ),
    )
    coef = []
    for c in range(3):
        half = slope[c] * 0.5
        coef.append((half, -half * pivot[c]))
    run[SLOTS] = jnp.zeros((4, RC, COLS), F32)
    table[...] = jnp.zeros_like(table)
    tag_land[tile] = tag_send[tile]
    pl.semaphore_wait(barrier, OWNERS + SLABS - 2)
    each(1, OWNERS, lambda j: tag_copy(j, tile).start())

    def render_and_send(chunk):
        def one(b):
            @pl.when(chunk == 0)
            def _():
                brick_copy(b).wait()

            render_rows(b, chunk, coef, res0, res1, bricks, samples, prints)

        each(0, BRICKS, one)

        def pick(i):
            stage[chunk, i] = prints[item_of[i]]

        each(0, SLOTS, pick)
        each(1, OWNERS, lambda j: tile_copy(chunk, j, tile).start())
        landed[chunk, pl.ds(2 * tile, 2)] = stage[chunk, pl.ds(2 * tile, 2)]

    each(0, CHUNKS, render_and_send)

    each(1, OWNERS, lambda j: tag_copy(j, source(j)).wait())
    depth_table(tag_land, table)
    scalars = pltpu.make_async_copy(table, table_s, table_sem)
    scalars.start()
    scalars.wait()

    def compose_and_send(chunk):
        each(1, OWNERS, lambda j: tile_copy(chunk, j, source(j)).wait())

        def keep(i):
            local[i] = landed[chunk, i]

        each(0, SLOTS, keep)

        def layer(p):
            x = local[table_s[0, p]].astype(F32)
            base = run[table_s[1, p]]
            shade = jnp.exp(-base[3])
            for c in range(3):
                run[p, c] = base[c] + x[c] * shade
            run[p, 3] = base[3] + x[3]

        each(0, SLOTS, layer)

        def close(t):
            pieces[chunk, t] = run[table_s[2, t]].astype(BF)

        each(0, TARGETS, close)
        each(1, SLABS, lambda e: slab_copy(chunk, e, slab).start())
        bands[chunk, pl.ds(2 * slab, 2)] = pieces[chunk, pl.ds(2 * slab, 2)]

    each(0, CHUNKS, compose_and_send)

    def blend(chunk):
        each(1, SLABS, lambda e: slab_copy(chunk, e, (slab - e + SLABS) % SLABS).wait())
        band[...] = bands[chunk]
        rows = pl.ds(pl.multiple_of(chunk * RC, RC), RC)
        for view in range(2):
            front = jnp.zeros((RC, COLS), F32)
            acc = [front] * 3
            for j in range(SLABS):
                x = band[chain[view * SLABS + j] * 2 + view].astype(F32)
                shade = jnp.exp(-front)
                for c in range(3):
                    acc[c] = acc[c] + shade * x[c]
                front = front + x[3]
            for c in range(3):
                colour[view, c, 0, rows, :] = acc[c]
            light_out[view, 0, rows, :] = jnp.exp(-front)

    each(0, CHUNKS, blend)


def body(volume, resampler, slope, pivot, tile_owner, tile_cell, depth_order, slab_rank):
    ids = jnp.arange(ITEMS)
    owner = tile_owner.reshape(-1)
    same = (owner[None, :] == owner[:, None]) & (ids[None, :] < ids[:, None])
    place = owner * 2 + jnp.sum(same.astype(I32), axis=1)
    view = jnp.tile(jnp.arange(2, dtype=I32), BRICKS)
    tag = depth_order.T.reshape(-1) * TARGETS + tile_cell.reshape(-1) * 2 + view
    hit = place[None, :] == jnp.arange(SLOTS, dtype=I32)[:, None]
    item_of = jnp.sum(jnp.where(hit, ids[None, :], 0), axis=1)
    slot_tag = jnp.min(jnp.where(hit, tag[None, :], EMPTY), axis=1).reshape(OWNERS, 1, 2)
    tag_send = jnp.broadcast_to(jnp.pad(slot_tag, ((0, 0), (0, 0), (0, 126))), (OWNERS, 8, 128))
    slabs = jnp.arange(SLABS, dtype=I32)
    chain = jnp.sum(
        jnp.where(slab_rank[:, None, :] == slabs[None, :, None], slabs[None, None, :], 0), axis=2
    ).reshape(-1)
    res0 = resampler[0]
    zero = jnp.zeros_like(res0)
    res1 = jnp.concatenate(
        [jnp.concatenate([resampler[1], zero], 1), jnp.concatenate([zero, resampler[1]], 1)], 0
    )
    smem = pl.BlockSpec(memory_space=pltpu.SMEM)
    vmem = pl.BlockSpec(memory_space=pltpu.VMEM)
    dma = pltpu.SemaphoreType.DMA
    return tuple(
        pl.pallas_call(
            kernel,
            in_specs=[smem, smem, smem, smem, vmem, vmem, vmem, pl.BlockSpec(memory_space=pl.ANY)],
            out_specs=[vmem, vmem],
            out_shape=[
                jax.ShapeDtypeStruct((2, 3, 1, ROWS, COLS), F32),
                jax.ShapeDtypeStruct((2, 1, ROWS, COLS), F32),
            ],
            scratch_shapes=[
                pltpu.VMEM((BRICKS, ROWS, ROWS, ROWS), BF),
                pltpu.VMEM((ITEMS, 4, RC, COLS), BF),
                pltpu.VMEM((64 * RC, COLS), F32),
                pltpu.VMEM((CHUNKS, SLOTS, 4, RC, COLS), BF),
                pltpu.VMEM((CHUNKS, SLOTS, 4, RC, COLS), BF),
                pltpu.VMEM((SLOTS, 4, RC, COLS), BF),
                pltpu.VMEM((SLOTS + 1, 4, RC, COLS), F32),
                pltpu.VMEM((CHUNKS, TARGETS, 4, RC, COLS), BF),
                pltpu.VMEM((CHUNKS, TARGETS, 4, RC, COLS), BF),
                pltpu.VMEM((TARGETS, 4, RC, COLS), BF),
                pltpu.VMEM((OWNERS, 8, 128), I32),
                pltpu.VMEM((8, 128), I32),
                pltpu.SMEM((8, 128), I32),
                dma((BRICKS,)),
                dma((CHUNKS, OWNERS)),
                dma((CHUNKS, OWNERS)),
                dma((CHUNKS, SLABS)),
                dma((CHUNKS, SLABS)),
                dma((OWNERS,)),
                dma((OWNERS,)),
                dma(()),
            ],
            compiler_params=pltpu.CompilerParams(
                collective_id=0, has_side_effects=True, vmem_limit_bytes=52 << 20
            ),
            name="composite",
        )(item_of, chain, slope, pivot, tag_send, res0, res1, volume)
    )


def solution(mesh):
    in_specs = (
        P(("depth", "tile"), None, None, None),
        P(),
        P(),
        P(),
        P(("depth", "tile"), None),
        P(("depth", "tile"), None),
        P(None, ("depth", "tile")),
        P(),
    )
    out_specs = (P(None, None, "tile", "depth", None), P(None, "tile", "depth", None))
    return jax.shard_map(body, mesh=mesh, in_specs=in_specs, out_specs=out_specs, check_vma=False)
```

time: 221 us -> 137 us (0.62)
  starting transfers between devices: 66.4 us -> 0 us
  Pallas kernels: 79.3 us -> 130 us
  waiting for transfers between devices: 39.7 us -> 0 us
  local copies, waits for them, and re-layouts: 29.5 us -> 4.58 us
    all_to_all x9 -> x0, starting transfers between devices: 66.4 us -> none  [the longest x4 32.5 us: body(): lax.all_to_all(sent.reshape(OWNERS, 2, 4, RC, COLS), 'tile', split_axis=0...]
    pallas_call x9 -> x1, Pallas kernels: 79.3 us -> 130 us  [body(): pl.pallas_call(kernel, in_specs=[smem, smem, smem, smem, vmem, vmem, vmem...]
    all_to_all x9 -> x0, waiting for transfers between devices: 39.7 us -> none  [the longest x4 22.8 us: body(): lax.all_to_all(sent.reshape(OWNERS, 2, 4, RC, COLS), 'tile', split_axis=0...]
    unnamed x23 -> x7, local copies, waits for them, and re-layouts: 27.1 us -> 3.37 us
  transfers between devices with their start and end apart: 9 -> 0, of which waited for: 8 -> 0; matrix products, arithmetic and copies ran while one was open for 1% -> 0% of each run, Pallas kernels for 36% -> 0%
where the time goes in v2:
time: 137 us
  Pallas kernels  130 us (95%)
  local copies, waits for them, and re-layouts  4.58 us (3%)
  other arithmetic  1.81 us (1%)
    pallas_call x1, Pallas kernels, body(): pl.pallas_call(kernel, in_specs=[smem, smem, smem, smem, vmem, vmem, vmem...  130 us
    unnamed x7, local copies, waits for them, and re-layouts  3.37 us

profile of v2, /device:TPU:33, one launch (start us, length us, event | category | flops | bytes accessed | tf_op | source)
XLA Modules:
  0.0 136.6 jit_solution(7241662039917571740)
XLA Ops:
  0.6 0.7 fusion.4
  1.3 0.8 select_reduce_fusion.2
  2.2 0.1 reshape.53.chain
  2.2 0.1 copy.15
  2.3 0.1 add.34
  2.4 0.8 copy.14
  3.2 0.1 reshape.52
  3.3 0.2 convert_reduce_fusion
  3.5 0.1 select_reduce_fusion
  3.6 0.1 reshape.54
  3.7 0.7 slice_bitcast_fusion
  4.4 0.0 copy-start
  4.5 0.6 copy-done
  5.1 0.0 copy-start.1
  5.1 0.7 copy-done.1
  5.8 129.5 %composite.1 = (f32[2,3,1,64,128]{4,3,2,1,0:T(8,128)S(1)}, f32[2,1,64,128]{3,2,1,0:T(8,128)S(1)}) custom-call(s32[64]{0:T(128)S(1)} %get-tuple-element.3.item_of, s32[16]{0:T(128)S(1)} %reshape.53.chain, f32[3]{0:T(128)S(1)} %copy-done, f32[3]{0:T(128)S(1)} %copy-done.1, s32[32,8,128]{2,1,0:T(8,128)S(1)} %broadcast_in_dim.56.tag_send, ...), custom_call_target="tpu_custom_call" | custom-call | tf_op jit(solution)/shard_map/composite/pallas_call | solution.py:295
  135.3 0.7 copy.18
  136.0 0.6 copy.19
  (4 shorter events, 0.0 us)
Async XLA Ops:
  4.4 0.7 copy-start
  5.1 0.7 copy-start.1

commit v3 on v2

--- a/solution.py
+++ b/solution.py
@@ -21,58 +21,63 @@
 RC = 16
 CHUNKS = ROWS // RC
 EMPTY = 1 << 20
+UNROLL = 8
+BLOCK = 7 * RC
 EXP_SCALE = -1.4426950408889634 / 64.0
 
 
-def march(samples_of, coef, write):
+SAMPLE_SCRATCH = [pltpu.VMEM((64 * RC, COLS), F32), pltpu.VMEM((64 * RC, COLS), F32)]
+HALF = RC // 2
+
+
+def prepare(brick, chunk, pair, wide, bricks, samples, thick):
+    top = pl.multiple_of(chunk * RC, RC)
+    x = jnp.concatenate([bricks[brick, top + pair], bricks[brick, top + pair + HALF]], axis=0)
+    y = lax.dot_general(x, wide[1], (((0,), (0,)), ((), ())), preferred_element_type=F32)
+    samples[pl.ds(pair, 64, stride=RC), :] = y[:, :COLS]
+    samples[pl.ds(pair + HALF, 64, stride=RC), :] = y[:, COLS:]
+    ones = jnp.ones((8, ROWS), BF)
+    total = lax.dot_general(ones, x, (((1,), (1,)), ((), ())), preferred_element_type=F32)
+    thick[pl.ds(pair, 1), :] = total[0:1]
+
+
+def march(brick, chunk, next_brick, next_chunk, coef, res, wide, bricks, prints, sums, now, later):
+    samples, other = now
+    top = pl.multiple_of(chunk * RC, RC)
     zero = jnp.zeros((RC, COLS), F32)
+    start = (zero, zero + 1.0, zero, zero, zero)
 
     def step(block, carry):
-        front, light, a0, a1, a2 = carry
-        acc = [a0, a1, a2]
-        rows = samples_of(block)
+        thick, *views = carry
+        cube = bricks[brick, pl.ds(block * 8, 8), pl.ds(top, RC), :]
+        x = cube.reshape(8 * RC, ROWS)
+        rows = [
+            jnp.dot(x, res[0], preferred_element_type=F32).reshape(8, RC, COLS),
+            samples[pl.ds(block * 8 * RC, 8 * RC), :].reshape(8, RC, COLS),
+        ]
+        thick = thick + jnp.sum(cube.astype(F32), axis=0)
+        prepare(next_brick, next_chunk, block, wide, bricks, *later)
         for j in range(8):
-            s = rows[j]
-            front = front + s
-            after = jnp.exp2(front * EXP_SCALE)
-            weight = light - after
-            light = after
-            for c in range(3):
-                acc[c] = acc[c] + weight * jnp.tanh(s * coef[c][0] + coef[c][1])
-        return (front, light, *acc)
-
-    front, light, a0, a1, a2 = lax.fori_loop(0, 8, step, (zero, zero + 1.0, zero, zero, zero), unroll=8)
-    total = 1.0 - light
-    for c, acc in enumerate((a0, a1, a2)):
-        write(c, (0.5 * (total + acc)).astype(BF))
-    write(3, (front * (1.0 / 64.0)).astype(BF))
-
-
-def render_rows(brick, chunk, coef, res0, res1, bricks, samples, prints):
-    top = pl.multiple_of(chunk * RC, RC)
-
-    def samples0(block):
-        x = bricks[brick, pl.ds(block * 8, 8), pl.ds(top, RC), :].reshape(8 * RC, ROWS)
-        return jnp.dot(x, res0[...], preferred_element_type=F32).reshape(8, RC, COLS)
-
-    def write0(c, x):
-        prints[2 * brick, c] = x
-
-    march(samples0, coef, write0)
-    half = RC // 2
-    for r in range(half):
-        x = jnp.concatenate([bricks[brick, top + r], bricks[brick, top + r + half]], axis=0)
-        y = lax.dot_general(x, res1[...], (((0,), (0,)), ((), ())), preferred_element_type=F32)
-        samples[pl.ds(r, 64, stride=RC), :] = y[:, :COLS]
-        samples[pl.ds(r + half, 64, stride=RC), :] = y[:, COLS:]
-
-    def samples1(block):
-        return samples[pl.ds(block * 8 * RC, 8 * RC), :].reshape(8, RC, COLS)
-
-    def write1(c, x):
-        prints[2 * brick + 1, c] = x
-
-    march(samples1, coef, write1)
+            for view in range(2):
+                front, light, *acc = views[view]
+                s = rows[view][j]
+                front = front + s
+                after = jnp.exp2(front * EXP_SCALE)
+                weight = light - after
+                for c in range(3):
+                    acc[c] = acc[c] + weight * jnp.tanh(s * coef[c][0] + coef[c][1])
+                views[view] = (front, after, *acc)
+        return (thick, *views)
+
+    thick, *views = lax.fori_loop(
+        0, 8, step, (jnp.zeros((RC, ROWS), F32), start, start), unroll=UNROLL
+    )
+    sums[2 * brick] = jnp.concatenate([thick[:HALF], thick[HALF:]], axis=1)
+    sums[2 * brick + 1] = other[...]
+    for view in range(2):
+        _, light, *acc = views[view]
+        for c in range(3):
+            prints[2 * brick + view, pl.ds(c * RC, RC), :] = (0.5 * ((1.0 - light) + acc[c])).astype(BF)
 
 
 def depth_table(tag_land, table):
@@ -107,12 +112,13 @@
     table[0:1, 0:SLOTS] = order
     table[1:2, 0:SLOTS] = prev
     table[2:3, 0:SLOTS] = last
+    table[3:4, 0:SLOTS] = (sorted_row[0:1] // SLOTS) % 2
 
 
 def kernel(
-    item_of, chain, slope, pivot, tag_send, res0, res1, volume,
+    item_of, chain, slope, pivot, tag_send, res, volume,
     colour, light_out,
-    bricks, prints, samples, stage, landed, local, run, pieces, bands, band, tag_land, table, table_s,
+    wide, bricks, prints, sums, samples_a, samples_b, thick_a, thick_b, stage, landed, local, depths, run, pieces, bands, band, tag_land, table, table_s,
     vol_sem, send_sem, recv_sem, out_sem, in_sem, tag_out, tag_in, table_sem,
 ):
     slab = lax.axis_index("depth")
@@ -136,8 +142,8 @@
 
     def tile_copy(chunk, j, land):
         return pltpu.make_async_remote_copy(
-            src_ref=stage.at[chunk, pl.ds(2 * peer(j), 2)],
-            dst_ref=landed.at[chunk, pl.ds(2 * land, 2)],
+            src_ref=stage.at[chunk, peer(j)],
+            dst_ref=landed.at[chunk, land],
             send_sem=send_sem.at[chunk, j],
             recv_sem=recv_sem.at[chunk, j],
             device_id={"tile": peer(j)},
@@ -190,28 +196,51 @@
     for c in range(3):
         half = slope[c] * 0.5
         coef.append((half, -half * pivot[c]))
+    wide[...] = jnp.zeros_like(wide)
+    for view in range(2):
+        wide[view, 0:ROWS, 0:COLS] = res[view]
+        wide[view, ROWS : 2 * ROWS, COLS : 2 * COLS] = res[view]
     run[SLOTS] = jnp.zeros((4, RC, COLS), F32)
     table[...] = jnp.zeros_like(table)
     tag_land[tile] = tag_send[tile]
     pl.semaphore_wait(barrier, OWNERS + SLABS - 2)
     each(1, OWNERS, lambda j: tag_copy(j, tile).start())
 
+    even, odd = (samples_a, thick_a), (samples_b, thick_b)
+    brick_copy(0).wait()
+    each(0, HALF, lambda pair: prepare(0, 0, pair, wide, bricks, *even))
+
     def render_and_send(chunk):
         def one(b):
+            shared = (coef, res, wide, bricks, prints, sums)
+            first, second = 2 * b, 2 * b + 1
+
             @pl.when(chunk == 0)
             def _():
-                brick_copy(b).wait()
-
-            render_rows(b, chunk, coef, res0, res1, bricks, samples, prints)
-
-        each(0, BRICKS, one)
-
-        def pick(i):
-            stage[chunk, i] = prints[item_of[i]]
-
-        each(0, SLOTS, pick)
+                brick_copy(second).wait()
+
+            march(first, chunk, second, chunk, *shared, even, odd)
+            wrap = second // (BRICKS - 1)
+
+            @pl.when((chunk == 0) & (b < BRICKS // 2 - 1))
+            def _():
+                brick_copy(second + 1).wait()
+
+            march(
+                second, chunk, (second + 1) % BRICKS, (chunk + wrap) % CHUNKS, *shared, odd, even
+            )
+
+        each(0, BRICKS // 2, one)
+
+        def pick(o):
+            one, two = item_of[2 * o], item_of[2 * o + 1]
+            stage[chunk, o, 0 : 3 * RC, :] = prints[one]
+            stage[chunk, o, 3 * RC : 6 * RC, :] = prints[two]
+            stage[chunk, o, 6 * RC : BLOCK, :] = jnp.concatenate([sums[one], sums[two]], axis=0).astype(BF)
+
+        each(0, OWNERS, pick)
         each(1, OWNERS, lambda j: tile_copy(chunk, j, tile).start())
-        landed[chunk, pl.ds(2 * tile, 2)] = stage[chunk, pl.ds(2 * tile, 2)]
+        landed[chunk, tile] = stage[chunk, tile]
 
     each(0, CHUNKS, render_and_send)
 
@@ -224,18 +253,27 @@
     def compose_and_send(chunk):
         each(1, OWNERS, lambda j: tile_copy(chunk, j, source(j)).wait())
 
-        def keep(i):
-            local[i] = landed[chunk, i]
-
-        each(0, SLOTS, keep)
+        def keep(g):
+            for i in range(8):
+                src = g * 8 + i
+                local[2 * src] = landed[chunk, src, 0 : 3 * RC, :]
+                local[2 * src + 1] = landed[chunk, src, 3 * RC : 6 * RC, :]
+            x = landed[chunk, pl.ds(g * 8, 8), 6 * RC : BLOCK, :].reshape(8 * RC, 2 * ROWS)
+            for view in range(2):
+                d = jnp.dot(x, wide[view], preferred_element_type=F32)
+                depths[view, pl.ds(16 * g, 16)] = (d * (1.0 / 64.0)).reshape(16, HALF, 2 * COLS)
+
+        each(0, OWNERS // 8, keep)
 
         def layer(p):
-            x = local[table_s[0, p]].astype(F32)
+            slot = table_s[0, p]
+            x = local[slot].astype(F32)
+            d = depths[table_s[3, p], slot]
             base = run[table_s[1, p]]
             shade = jnp.exp(-base[3])
+            run[p, 3] = base[3] + jnp.concatenate([d[:, :COLS], d[:, COLS:]], axis=0)
             for c in range(3):
-                run[p, c] = base[c] + x[c] * shade
-            run[p, 3] = base[3] + x[3]
+                run[p, c] = base[c] + x[c * RC : (c + 1) * RC] * shade
 
         each(0, SLOTS, layer)
 
@@ -283,30 +321,30 @@
     chain = jnp.sum(
         jnp.where(slab_rank[:, None, :] == slabs[None, :, None], slabs[None, None, :], 0), axis=2
     ).reshape(-1)
-    res0 = resampler[0]
-    zero = jnp.zeros_like(res0)
-    res1 = jnp.concatenate(
-        [jnp.concatenate([resampler[1], zero], 1), jnp.concatenate([zero, resampler[1]], 1)], 0
-    )
     smem = pl.BlockSpec(memory_space=pltpu.SMEM)
     vmem = pl.BlockSpec(memory_space=pltpu.VMEM)
     dma = pltpu.SemaphoreType.DMA
     return tuple(
         pl.pallas_call(
             kernel,
-            in_specs=[smem, smem, smem, smem, vmem, vmem, vmem, pl.BlockSpec(memory_space=pl.ANY)],
+            in_specs=[smem, smem, smem, smem, vmem, vmem, pl.BlockSpec(memory_space=pl.ANY)],
             out_specs=[vmem, vmem],
             out_shape=[
                 jax.ShapeDtypeStruct((2, 3, 1, ROWS, COLS), F32),
                 jax.ShapeDtypeStruct((2, 1, ROWS, COLS), F32),
             ],
             scratch_shapes=[
+                pltpu.VMEM((2, 2 * ROWS, 2 * COLS), BF),
                 pltpu.VMEM((BRICKS, ROWS, ROWS, ROWS), BF),
-                pltpu.VMEM((ITEMS, 4, RC, COLS), BF),
-                pltpu.VMEM((64 * RC, COLS), F32),
-                pltpu.VMEM((CHUNKS, SLOTS, 4, RC, COLS), BF),
-                pltpu.VMEM((CHUNKS, SLOTS, 4, RC, COLS), BF),
-                pltpu.VMEM((SLOTS, 4, RC, COLS), BF),
+                pltpu.VMEM((ITEMS, 3 * RC, COLS), BF),
+                pltpu.VMEM((ITEMS, HALF, 2 * ROWS), F32),
+                *SAMPLE_SCRATCH,
+                pltpu.VMEM((HALF, 2 * ROWS), F32),
+                pltpu.VMEM((HALF, 2 * ROWS), F32),
+                pltpu.VMEM((CHUNKS, OWNERS, BLOCK, COLS), BF),
+                pltpu.VMEM((CHUNKS, OWNERS, BLOCK, COLS), BF),
+                pltpu.VMEM((SLOTS, 3 * RC, COLS), BF),
+                pltpu.VMEM((2, SLOTS, HALF, 2 * COLS), F32),
                 pltpu.VMEM((SLOTS + 1, 4, RC, COLS), F32),
                 pltpu.VMEM((CHUNKS, TARGETS, 4, RC, COLS), BF),
                 pltpu.VMEM((CHUNKS, TARGETS, 4, RC, COLS), BF),
@@ -327,7 +365,7 @@
                 collective_id=0, has_side_effects=True, vmem_limit_bytes=52 << 20
             ),
             name="composite",
-        )(item_of, chain, slope, pivot, tag_send, res0, res1, volume)
+        )(item_of, chain, slope, pivot, tag_send, resampler, volume)
     )
 
 

time: 137 us -> 127 us (0.927)
  Pallas kernels: 130 us -> 119 us
    pallas_call x1, Pallas kernels: 130 us -> 119 us  [body(): pl.pallas_call(kernel, in_specs=[smem, smem, smem, smem, vmem, vmem, pl.B...]
    unnamed x7 -> x9, local copies, waits for them, and re-layouts: 3.37 us -> 4.13 us
where the time goes in v3:
time: 127 us; the launch traced here: 126 us
  Pallas kernels  119 us (94%)
  local copies, waits for them, and re-layouts  4.59 us (4%)
  other arithmetic  1.8 us (1%)
    pallas_call x1, Pallas kernels, body(): pl.pallas_call(kernel, in_specs=[smem, smem, smem, smem, vmem, vmem, pl.B...  119 us
    unnamed x9, local copies, waits for them, and re-layouts  4.13 us

profile of v3, /device:TPU:33, one launch (start us, length us, event | category | flops | bytes accessed | tf_op | source)
XLA Modules:
  0.0 126.4 jit_solution(10218577710984631149)
XLA Ops:
  0.6 0.7 fusion.1
  1.3 0.8 select_reduce_fusion.2
  2.2 0.1 reshape.53.chain
  2.2 0.1 copy.15
  2.3 0.1 add.30
  2.4 0.8 copy.14
  3.2 0.1 reshape.52
  3.3 0.2 convert_reduce_fusion
  3.5 0.1 select_reduce_fusion
  3.6 0.1 reshape.54
  3.7 0.0 copy-start
  3.7 0.7 copy-done
  4.5 0.0 copy-start.1
  4.5 0.7 copy-done.1
  5.1 0.0 copy-start.2
  5.1 0.7 copy-done.2
  5.8 119.3 %composite.1 = (f32[2,3,1,64,128]{4,3,2,1,0:T(8,128)S(1)}, f32[2,1,64,128]{3,2,1,0:T(8,128)S(1)}) custom-call(s32[64]{0:T(128)S(1)} %get-tuple-element.3.item_of, s32[16]{0:T(128)S(1)} %reshape.53.chain, f32[3]{0:T(128)S(1)} %copy-done.1, f32[3]{0:T(128)S(1)} %copy-done.2, s32[32,8,128]{2,1,0:T(8,128)S(1)} %broadcast_in_dim.55.tag_send, ...), custom_call_target="tpu_custom_call" | custom-call | tf_op jit(solution)/shard_map/composite/pallas_call | solution.py:328
  125.1 0.7 copy.18
  125.8 0.6 copy.19
  (3 shorter events, 0.0 us)
Async XLA Ops:
  3.7 0.8 copy-start
  4.5 0.7 copy-start.1
  5.1 0.7 copy-start.2

commit v4 on v3

--- a/solution.py
+++ b/solution.py
@@ -125,17 +125,20 @@
     tile = lax.axis_index("tile")
     z, y = tile // NY, tile % NY
 
+    planes = [(z + dz) % NZ for dz in range(NZ)]
+    columns = [(y + dy) % NY for dy in range(NY)]
+
     def hop(j):
         m = j // NY
         return (2 * (m % 2) - 1) * ((m + 1) // 2), j % NY
 
     def peer(j):
         dz, dy = hop(j)
-        return ((z + dz + NZ) % NZ) * NY + (y + dy) % NY
+        return planes[dz % NZ] * NY + columns[dy]
 
     def source(j):
         dz, dy = hop(j)
-        return ((z - dz + NZ) % NZ) * NY + (y - dy + NY) % NY
+        return planes[-dz % NZ] * NY + columns[-dy % NY]
 
     def brick_copy(b):
         return pltpu.make_async_copy(volume.at[b], bricks.at[b], vol_sem.at[b])
@@ -178,11 +181,13 @@
 
         lax.fori_loop(low, high, step, 0)
 
+    def every(do):
+        for j in range(1, OWNERS):
+            do(j)
+
     each(0, BRICKS, lambda b: brick_copy(b).start())
     barrier = pltpu.get_barrier_semaphore()
-    each(
-        1,
-        OWNERS,
+    every(
         lambda j: pl.semaphore_signal(barrier, inc=1, device_id={"tile": peer(j)}, device_id_type=MESH),
     )
     each(
@@ -204,7 +209,7 @@
     table[...] = jnp.zeros_like(table)
     tag_land[tile] = tag_send[tile]
     pl.semaphore_wait(barrier, OWNERS + SLABS - 2)
-    each(1, OWNERS, lambda j: tag_copy(j, tile).start())
+    every(lambda j: tag_copy(j, tile).start())
 
     even, odd = (samples_a, thick_a), (samples_b, thick_b)
     brick_copy(0).wait()
@@ -239,19 +244,19 @@
             stage[chunk, o, 6 * RC : BLOCK, :] = jnp.concatenate([sums[one], sums[two]], axis=0).astype(BF)
 
         each(0, OWNERS, pick)
-        each(1, OWNERS, lambda j: tile_copy(chunk, j, tile).start())
+        every(lambda j: tile_copy(chunk, j, tile).start())
         landed[chunk, tile] = stage[chunk, tile]
 
     each(0, CHUNKS, render_and_send)
 
-    each(1, OWNERS, lambda j: tag_copy(j, source(j)).wait())
+    every(lambda j: tag_copy(j, source(j)).wait())
     depth_table(tag_land, table)
     scalars = pltpu.make_async_copy(table, table_s, table_sem)
     scalars.start()
     scalars.wait()
 
     def compose_and_send(chunk):
-        each(1, OWNERS, lambda j: tile_copy(chunk, j, source(j)).wait())
+        every(lambda j: tile_copy(chunk, j, source(j)).wait())
 
         def keep(g):
             for i in range(8):

time: 127 us -> 125 us (0.984)
    pallas_call x1, Pallas kernels: 119 us -> 118 us  [body(): pl.pallas_call(kernel, in_specs=[smem, smem, smem, smem, vmem, vmem, pl.B...]
where the time goes in v4:
time: 125 us
  Pallas kernels  118 us (94%)
  local copies, waits for them, and re-layouts  4.59 us (4%)
  other arithmetic  1.8 us (1%)
    pallas_call x1, Pallas kernels, body(): pl.pallas_call(kernel, in_specs=[smem, smem, smem, smem, vmem, vmem, pl.B...  118 us
    unnamed x9, local copies, waits for them, and re-layouts  4.13 us

profile of v4, /device:TPU:33, one launch (start us, length us, event | category | flops | bytes accessed | tf_op | source)
XLA Modules:
  0.0 124.9 jit_solution(16816916741956357107)
XLA Ops:
  0.6 0.7 fusion.1
  1.3 0.8 select_reduce_fusion.2
  2.2 0.1 reshape.53.chain
  2.2 0.1 copy.15
  2.3 0.1 add.30
  2.4 0.8 copy.14
  3.2 0.1 reshape.52
  3.3 0.2 convert_reduce_fusion
  3.5 0.1 select_reduce_fusion
  3.6 0.1 reshape.54
  3.7 0.0 copy-start
  3.7 0.7 copy-done
  4.5 0.0 copy-start.1
  4.5 0.7 copy-done.1
  5.1 0.0 copy-start.2
  5.1 0.7 copy-done.2
  5.8 117.8 %composite.1 = (f32[2,3,1,64,128]{4,3,2,1,0:T(8,128)S(1)}, f32[2,1,64,128]{3,2,1,0:T(8,128)S(1)}) custom-call(s32[64]{0:T(128)S(1)} %get-tuple-element.3.item_of, s32[16]{0:T(128)S(1)} %reshape.53.chain, f32[3]{0:T(128)S(1)} %copy-done.1, f32[3]{0:T(128)S(1)} %copy-done.2, s32[32,8,128]{2,1,0:T(8,128)S(1)} %broadcast_in_dim.55.tag_send, ...), custom_call_target="tpu_custom_call" | custom-call | tf_op jit(solution)/shard_map/composite/pallas_call | solution.py:333
  123.6 0.7 copy.18
  124.2 0.6 copy.19
  (3 shorter events, 0.0 us)
Async XLA Ops:
  3.7 0.8 copy-start
  4.5 0.7 copy-start.1
  5.1 0.7 copy-start.2

commit v5 on v4

--- a/solution.py
+++ b/solution.py
@@ -174,12 +174,12 @@
             device_id_type=MESH,
         )
 
-    def each(low, high, do):
+    def each(low, high, do, unroll=1):
         def step(i, _):
             do(i)
             return 0
 
-        lax.fori_loop(low, high, step, 0)
+        lax.fori_loop(low, high, step, 0, unroll=unroll)
 
     def every(do):
         for j in range(1, OWNERS):
@@ -280,12 +280,12 @@
             for c in range(3):
                 run[p, c] = base[c] + x[c * RC : (c + 1) * RC] * shade
 
-        each(0, SLOTS, layer)
+        each(0, SLOTS, layer, 4)
 
         def close(t):
             pieces[chunk, t] = run[table_s[2, t]].astype(BF)
 
-        each(0, TARGETS, close)
+        each(0, TARGETS, close, 4)
         each(1, SLABS, lambda e: slab_copy(chunk, e, slab).start())
         bands[chunk, pl.ds(2 * slab, 2)] = pieces[chunk, pl.ds(2 * slab, 2)]
 

time: 125 us -> 125 us (level)
  no operation moved by 1% of the time
where the time goes in v5:
time: 125 us
  Pallas kernels  118 us (94%)
  local copies, waits for them, and re-layouts  4.59 us (4%)
  other arithmetic  1.8 us (1%)
    pallas_call x1, Pallas kernels, body(): pl.pallas_call(kernel, in_specs=[smem, smem, smem, smem, vmem, vmem, pl.B...  118 us
    unnamed x9, local copies, waits for them, and re-layouts  4.13 us

profile of v5, /device:TPU:33, one launch (start us, length us, event | category | flops | bytes accessed | tf_op | source)
XLA Modules:
  0.0 124.7 jit_solution(684977168641275052)
XLA Ops:
  0.6 0.7 fusion.1
  1.3 0.8 select_reduce_fusion.2
  2.2 0.1 reshape.53.chain
  2.2 0.1 copy.15
  2.3 0.1 add.30
  2.4 0.8 copy.14
  3.2 0.1 reshape.52
  3.3 0.2 convert_reduce_fusion
  3.5 0.1 select_reduce_fusion
  3.6 0.1 reshape.54
  3.7 0.0 copy-start
  3.7 0.7 copy-done
  4.5 0.0 copy-start.1
  4.5 0.7 copy-done.1
  5.1 0.0 copy-start.2
  5.1 0.7 copy-done.2
  5.8 117.6 %composite.1 = (f32[2,3,1,64,128]{4,3,2,1,0:T(8,128)S(1)}, f32[2,1,64,128]{3,2,1,0:T(8,128)S(1)}) custom-call(s32[64]{0:T(128)S(1)} %get-tuple-element.3.item_of, s32[16]{0:T(128)S(1)} %reshape.53.chain, f32[3]{0:T(128)S(1)} %copy-done.1, f32[3]{0:T(128)S(1)} %copy-done.2, s32[32,8,128]{2,1,0:T(8,128)S(1)} %broadcast_in_dim.55.tag_send, ...), custom_call_target="tpu_custom_call" | custom-call | tf_op jit(solution)/shard_map/composite/pallas_call | solution.py:333
  123.4 0.7 copy.18
  124.1 0.6 copy.19
  (3 shorter events, 0.0 us)
Async XLA Ops:
  3.7 0.8 copy-start
  4.5 0.7 copy-start.1
  5.1 0.7 copy-start.2
